TPU v7x, 512 devices: a whole 4x8x8 slice. The times are simulated.
512 devices in a mesh: seq: 128 (over y, z, core), head: 4 (over x).
Axes of the slice: x: 4, y: 8, z: 8, core: 2. Of those that a mesh axis runs over, the one named last changes fastest.
Arguments:
- queries: bfloat16 [65536, 4096], P('seq', 'head'), may hold values from -7 to 7
- keys: bfloat16 [65536, 1024], P('seq', 'head'), may hold values from -5 to 5
- values: bfloat16 [65536, 1024], P('seq', 'head'), may hold values from -6 to 6
- picks: int32 [65536, 2], P('seq'), may hold values from -1 to 126, as said below
- out_weight: bfloat16 [4096, 4096], P('seq', 'head'), may hold values from -0.09375 to 0.09375
Outputs:
- mixed: bfloat16 [65536, 4096], P('seq', 'head')
Inputs may be any that keep to these rules, and one draw needn't show every extreme that they name: `picks`: for the tokens of block d, every entry is -1 or a block number below d; a row's two entries differ unless both are -1; a row naming one block has it first, and a row naming two has the lower first; each earlier block is named by exactly 6 of block d's rows.
All inputs are finite; a program needn't handle non-finite values.
Results may differ from a plain program's by a relative error of at most 0.0054.
Values may be sent and summed in bfloat16 or wider, within the bound.
A program may use at most 64 MiB of HBM per device.

v0:
```python
import math

import jax
import jax.numpy as jnp
from jax import lax
from jax.sharding import PartitionSpec as P

HEAD_SIZE = 128
CAP = 6


NEG_FILL = -1e30


def own_partial(query_matrix, key_matrix, value_matrix, score_scale):
    row_count = query_matrix.shape[0]
    key_count = key_matrix.shape[0]
    scores = (
        jnp.einsum("qjgd,kjd->jgqk", query_matrix, key_matrix, preferred_element_type=jnp.float32)
        * score_scale
    )
    visible = jnp.arange(key_count)[None, :] <= jnp.arange(row_count)[:, None]
    scores = jnp.where(visible, scores, NEG_FILL)
    peak_score = jnp.max(scores, axis=-1)
    weights = jnp.where(visible, jnp.exp(scores - peak_score[..., None]), 0.0)
    totals = jnp.sum(weights, axis=-1)
    mixed_rows = jnp.einsum(
        "jgqk,kjd->qjgd",
        weights.astype(jnp.bfloat16),
        value_matrix,
        preferred_element_type=jnp.float32,
    )
    mixed_rows = mixed_rows / jnp.transpose(totals, (2, 0, 1))[..., None]
    return (
        mixed_rows.reshape(row_count, -1, HEAD_SIZE),
        jnp.transpose(peak_score, (2, 0, 1)).reshape(row_count, -1),
        jnp.transpose(totals, (2, 0, 1)).reshape(row_count, -1),
    )


def merge_parts(own_out, own_peak, own_total, pick_out, pick_peak, pick_total, live_rows):
    live_mask = live_rows[:, :, None]
    pick_peak = jnp.where(live_mask, pick_peak, own_peak[:, None, :])
    summit = jnp.maximum(own_peak, jnp.max(pick_peak, axis=1))
    own_weight = own_total * jnp.exp(own_peak - summit)
    pick_weight = jnp.where(live_mask, pick_total * jnp.exp(pick_peak - summit[:, None, :]), 0.0)
    weighted_sum = own_weight[..., None] * own_out + jnp.sum(
        pick_weight[..., None] * pick_out, axis=1
    )
    return weighted_sum / (own_weight + jnp.sum(pick_weight, axis=1))[..., None]


def on_device(queries, keys, values, picks, out_weight):
    owner_count = lax.axis_size("seq")
    block_len = queries.shape[0]
    kv_local = keys.shape[1] // HEAD_SIZE
    heads_local = queries.shape[1] // HEAD_SIZE
    heads_per_group = heads_local // kv_local
    score_scale = 1.0 / math.sqrt(HEAD_SIZE)
    slot_count_total = owner_count * CAP
    flat_picks = picks.reshape(-1)
    owner_ids = jnp.arange(owner_count, dtype=jnp.int32)
    matches = (flat_picks[:, None] == owner_ids[None, :]).astype(jnp.int32)
    pick_rank = jnp.sum((jnp.cumsum(matches, axis=0) - 1) * matches, axis=1)
    is_live = flat_picks >= 0
    slot_index = jnp.where(is_live, flat_picks * CAP + pick_rank, slot_count_total)
    slot_rows = (
        jnp.zeros((slot_count_total,), jnp.int32)
        .at[slot_index]
        .set(jnp.arange(2 * block_len, dtype=jnp.int32) // 2, mode="drop")
    )
    outgoing = queries[slot_rows].reshape(owner_count, CAP, queries.shape[1])
    key_heads = keys.reshape(block_len, kv_local, HEAD_SIZE)
    value_heads = values.reshape(block_len, kv_local, HEAD_SIZE)
    arrived = lax.all_to_all(outgoing, "seq", split_axis=0, concat_axis=0, tiled=True)
    sources, slot_width, features = arrived.shape
    query_matrix = arrived.reshape(sources * slot_width, kv_local, heads_per_group, HEAD_SIZE)
    scores = (
        jnp.einsum("sjgd,kjd->jgsk", query_matrix, key_heads, preferred_element_type=jnp.float32)
        * score_scale
    )
    peak_score = jnp.max(scores, axis=-1)
    weights = jnp.exp(scores - peak_score[..., None])
    totals = jnp.sum(weights, axis=-1)
    mixed_rows = jnp.einsum(
        "jgsk,kjd->sjgd",
        weights.astype(jnp.bfloat16),
        value_heads,
        preferred_element_type=jnp.float32,
    )
    mixed_rows = mixed_rows / jnp.transpose(totals, (2, 0, 1))[..., None]
    part_out = lax.all_to_all(
        mixed_rows.reshape(sources, slot_width, features),
        "seq",
        split_axis=0,
        concat_axis=0,
        tiled=True,
    )
    part_peak = lax.all_to_all(
        jnp.transpose(peak_score, (2, 0, 1)).reshape(sources, slot_width, heads_local),
        "seq",
        split_axis=0,
        concat_axis=0,
        tiled=True,
    )
    part_total = lax.all_to_all(
        jnp.transpose(totals, (2, 0, 1)).reshape(sources, slot_width, heads_local),
        "seq",
        split_axis=0,
        concat_axis=0,
        tiled=True,
    )
    safe_index = jnp.minimum(slot_index, slot_count_total - 1)
    pick_out = part_out.reshape(slot_count_total, heads_local, HEAD_SIZE)[safe_index].reshape(
        block_len, 2, heads_local, HEAD_SIZE
    )
    pick_peak = part_peak.reshape(slot_count_total, heads_local)[safe_index].reshape(
        block_len, 2, heads_local
    )
    pick_total = part_total.reshape(slot_count_total, heads_local)[safe_index].reshape(
        block_len, 2, heads_local
    )
    live_rows = is_live.reshape(block_len, 2)
    local_rows = queries.reshape(block_len, kv_local, heads_per_group, HEAD_SIZE)
    own_out, own_peak, own_total = own_partial(local_rows, key_heads, value_heads, score_scale)
    attention = merge_parts(
        own_out, own_peak, own_total, pick_out, pick_peak, pick_total, live_rows
    )
    attention = attention.reshape(block_len, heads_local * HEAD_SIZE).astype(jnp.bfloat16)
    every_head = lax.all_gather(attention, "head", axis=1, tiled=True)
    return jnp.dot(
        every_head,
        lax.all_gather(out_weight, "seq", axis=0, tiled=True),
        preferred_element_type=jnp.float32,
    ).astype(jnp.bfloat16)


def solution(mesh):
    return jax.shard_map(
        on_device,
        mesh=mesh,
        in_specs=(
            P("seq", "head"),
            P("seq", "head"),
            P("seq", "head"),
            P("seq", None),
            P("seq", "head"),
        ),
        out_specs=P("seq", "head"),
        check_vma=False,
    )
```

profile of v0, /device:TPU:1, one launch (start us, length us, event | category | flops | bytes accessed | tf_op | source)
XLA Modules:
  0.0 453.5 jit_solution(16219849159573719858)
XLA Ops:
  6.5 0.9 copy.99
  7.8 0.7 broadcast_compare_fusion
  8.5 0.7 broadcast_multiply_fusion
  10.4 0.4 fusion.22
  10.8 4.3 scatter_custom_fusion
  15.2 2.8 gather_fusion
  18.0 1.6 reshape.204
  19.6 18.4 %all-to-all-start = ((bf16[128,6,1024]{2,1,0:T(8,128)(2,1)}), bf16[128,6,1024]{2,1,0:T(8,128)(2,1)S(1)}, u32[]{:S(2)}, u32[]{:S(2)}) async-start(bf16[128,6,1024]{2,1,0:T(8,128)(2,1)} %reshape.204), calls=%async_computation | async-start | bytes 4194304 | tf_op jit(solution)/shard_map/all_to_all | solution.py:75
  38.0 1.0 reshape.199
  39.1 1.7 reshape.209
  40.8 1.8 copy.124
  42.6 47.6 %all-to-all-done = bf16[128,6,1024]{2,1,0:T(8,128)(2,1)S(1)} async-done(((bf16[128,6,1024]{2,1,0:T(8,128)(2,1)}), bf16[128,6,1024]{2,1,0:T(8,128)(2,1)S(1)}, u32[]{:S(2)}, u32[]{:S(2)}) %all-to-all-start) | async-done | bytes 1572896 | tf_op jit(solution)/shard_map/all_to_all | solution.py:75
  90.2 2.0 reshape.205
  92.2 7.8 %bitcast_reduce_fusion = (f32[2,4,768]{2,1,0:T(4,128)S(1)}, f32[2,768,4,512]{1,3,2,0:T(8,128)}) fusion(bf16[512,2,128,1]{2,1,0,3:T(2,128)(2,1)S(1)} %bitcast.81, bf16[768,2,4,128]{3,2,1,0:T(4,128)(2,1)} %reshape.205), kind=kOutput, calls=%fused_computation.6 | convolution fusion | flops 811591680 | bytes 14442496 | tf_op jit(solution)/shard_map/sjgd,kjd->jgsk/dot_general | solution.py:79
  100.0 0.5 reshape.206
  100.5 1.1 copy.105
  101.6 8.4 %all-to-all-start.1 = ((f32[128,6,8]{1,2,0:T(8,128)}), f32[128,6,8]{1,2,0:T(8,128)S(1)}, u32[]{:S(2)}, u32[]{:S(2)}) async-start(f32[128,6,8]{1,2,0:T(8,128)} %copy.105), calls=%async_computation.1 | async-start | bytes 1048576 | tf_op jit(solution)/shard_map/all_to_all | solution.py:99
  110.0 6.7 %fusion.2 = f32[2,4,768]{2,1,0:T(4,128)S(1)} fusion(f32[2,768,4,512]{1,3,2,0:T(8,128)} %get-tuple-element.12, f32[2,4,768]{2,1,0:T(4,128)S(1)} %get-tuple-element.11), kind=kLoop, calls=%fused_computation.9 | loop fusion | flops 9431040 | bytes 12632064 | tf_op jit(solution)/shard_map/reduce_sum | solution.py:84
  116.7 0.5 reshape.211
  117.2 1.1 copy.112
  118.3 11.0 %all-to-all-done.1 = f32[128,6,8]{1,2,0:T(8,128)S(1)} async-done(((f32[128,6,8]{1,2,0:T(8,128)}), f32[128,6,8]{1,2,0:T(8,128)S(1)}, u32[]{:S(2)}, u32[]{:S(2)}) %all-to-all-start.1) | async-done | bytes 24608 | tf_op jit(solution)/shard_map/all_to_all | solution.py:99
  129.3 7.2 %all-to-all-start.2 = ((f32[128,6,8]{1,2,0:T(8,128)}), f32[128,6,8]{1,2,0:T(8,128)S(1)}, u32[]{:S(2)}, u32[]{:S(2)}) async-start(f32[128,6,8]{1,2,0:T(8,128)} %copy.112), calls=%async_computation.2 | async-start | bytes 1048576 | tf_op jit(solution)/shard_map/all_to_all | solution.py:106
  136.6 6.6 %bitcast_divide_fusion = f32[768,2,4,128]{3,0,2,1:T(8,128)S(1)} fusion(bf16[512,2,128,1]{0,2,3,1:T(8,128)(2,1)S(1)} %copy-done.1, f32[2,768,4,512]{1,3,2,0:T(8,128)} %get-tuple-element.12, f32[2,4,768]{2,1,0:T(4,128)S(1)} %get-tuple-element.11, f32[768,2,4]{0,2,1:T(4,128)S(1)} %bitcast.86), kind=kOutput, calls=%fused_computation.21 | convolution fusion | flops 815529984 | bytes 16039936 | tf_op jit(solution)/shard_map/jgsk,kjd->sjgd/dot_general | solution.py:85
  143.2 3.7 copy.118
  146.9 5.0 %reshape.214 = f32[128,6,1024]{2,1,0:T(8,128)} reshape(f32[768,2,4,128]{3,2,1,0:T(4,128)} %copy.118) | data formatting | bytes 6291456 | tf_op jit(solution)/shard_map/reshape | solution.py:93
  152.0 4.2 all-to-all-done.2
  156.2 10.1 %all-to-all-start.3 = ((f32[128,6,1024]{2,1,0:T(8,128)}), f32[128,6,1024]{2,1,0:T(8,128)}, u32[]{:S(2)}, u32[]{:S(2)}) async-start(f32[128,6,1024]{2,1,0:T(8,128)} %reshape.214), calls=%async_computation.3 | async-start | bytes 8388608 | tf_op jit(solution)/shard_map/all_to_all | solution.py:92
  166.5 1.5 reshape.200
  168.1 6.1 %fusion.3 = (f32[2,4,512]{2,1,0:T(4,128)S(1)}, f32[2,512,512,4]{2,1,3,0:T(8,128)}) fusion(pred[512,512]{0,1:T(8,128)(4,1)S(1)} %iota_compare_fusion, bf16[512,2,4,128]{3,2,1,0:T(4,128)(2,1)} %reshape.200, bf16[512,2,128,1]{2,1,0,3:T(2,128)(2,1)S(1)} %bitcast.82), kind=kOutput, calls=%fused_computation.12 | convolution fusion | flops 543158272 | bytes 9977856 | tf_op jit(solution)/shard_map/qjgd,kjd->jgqk/dot_general | solution.py:19
  174.4 4.5 fusion.9
  178.9 7.3 %bitcast_divide_fusion.2 = f32[512,2,4,128]{0,3,2,1:T(8,128)} fusion(bf16[512,2,128,1]{0,2,3,1:T(8,128)(2,1)S(1)} %copy-done.1, f32[2,512,512,4]{2,1,3,0:T(8,128)} %get-tuple-element.14, f32[2,4,512]{2,1,0:T(4,128)S(1)} %get-tuple-element.13, pred[512,512]{0,1:T(8,128)(4,1)S(1)} %iota_compare_fusion, f32[512,2,4]{0,2,1:T(4,128)S(1)} %bitcast.89), kind=kOutput, calls=%fused_computation.26 | convolution fusion | flops 547880960 | bytes 11042816 | tf_op jit(solution)/shard_map/jgqk,kjd->qjgd/dot_general | solution.py:27
  186.2 0.8 copy.131
  187.1 2.8 gather_fusion.1
  189.9 3.4 fusion.25
  193.5 0.8 copy.134
  194.4 2.8 gather_fusion.2
  197.2 2.9 fusion.39
  200.3 61.5 %all-to-all-done.3 = f32[128,6,1024]{2,1,0:T(8,128)} async-done(((f32[128,6,1024]{2,1,0:T(8,128)}), f32[128,6,1024]{2,1,0:T(8,128)}, u32[]{:S(2)}, u32[]{:S(2)}) %all-to-all-start.3) | async-done | bytes 3145760 | tf_op jit(solution)/shard_map/all_to_all | solution.py:92
  261.8 4.8 %reshape.215 = f32[768,8,128]{2,1,0:T(8,128)} reshape(f32[128,6,1024]{2,1,0:T(8,128)} %all-to-all-done.3) | data formatting | bytes 6291456 | tf_op jit(solution)/shard_map/reshape | solution.py:114
  266.6 10.0 %gather_fusion.3 = f32[1024,8,128]{2,1,0:T(8,128)} fusion(f32[768,8,128]{2,1,0:T(8,128)} %reshape.215, s32[1024]{0:T(1024)S(1)} %broadcast_clamp_fusion), kind=kCustom, calls=%fused_computation.3 | custom fusion | bytes 8392704 | tf_op jit(solution)/shard_map/gather | solution.py:114
  276.7 4.3 multiply_reduce_fusion
  281.0 1.9 copy.137
  282.9 3.1 fusion.13
  286.1 0.3 all-gather.5.cloned.1.call-start
  286.4 0.5 all-gather.5.cloned.1.call-update
  286.8 57.3 %all-gather.3.cloned.1.call-done = bf16[512,4096]{0,1:T(8,128)(2,1)} async-done(((bf16[512,1024]{0,1:T(8,128)(2,1)}), bf16[512,4096]{0,1:T(8,128)(2,1)}) %all-gather.3.cloned.1.call-update) | async-done | bytes 4194320 | tf_op jit(solution)/shard_map/all_gather | solution.py:130
  344.2 92.1 %all-gather.5.cloned.1.call-done = bf16[4096,1024]{1,0:T(8,128)(2,1)} async-done(((bf16[32,1024]{1,0:T(8,128)(2,1)}), bf16[4096,1024]{1,0:T(8,128)(2,1)}) %all-gather.5.cloned.1.call-update) | async-done | bytes 8388624 | tf_op jit(solution)/shard_map/all_gather | solution.py:133
  436.3 10.1 %convolution_convert_fusion = bf16[512,1024]{1,0:T(8,128)(2,1)} fusion(bf16[512,4096]{0,1:T(8,128)(2,1)} %all-gather.3.cloned.1.call-done, bf16[4096,1024]{1,0:T(8,128)(2,1)} %all-gather.5.cloned.1.call-done), kind=kOutput, calls=%fused_computation.29 | convolution fusion | flops 4295491584 | bytes 13631488 | tf_op jit(solution)/shard_map/dot_general | solution.py:131
  (35 shorter events, 2.5 us)
Async XLA Ops:
  6.5 8.6 %copy-start = (bf16[512,1024]{1,0:T(8,128)(2,1)S(1)}, bf16[512,1024]{1,0:T(8,128)(2,1)}, u32[]{:S(2)}) copy-start(bf16[512,1024]{1,0:T(8,128)(2,1)} %param.5) | copy-start | bytes 3145732
  19.6 70.6 %all-to-all-start = ((bf16[128,6,1024]{2,1,0:T(8,128)(2,1)}), bf16[128,6,1024]{2,1,0:T(8,128)(2,1)S(1)}, u32[]{:S(2)}, u32[]{:S(2)}) async-start(bf16[128,6,1024]{2,1,0:T(8,128)(2,1)} %reshape.204), calls=%async_computation | async-start | bytes 4194304 | tf_op jit(solution)/shard_map/all_to_all | solution.py:75
  101.6 27.7 %all-to-all-start.1 = ((f32[128,6,8]{1,2,0:T(8,128)}), f32[128,6,8]{1,2,0:T(8,128)S(1)}, u32[]{:S(2)}, u32[]{:S(2)}) async-start(f32[128,6,8]{1,2,0:T(8,128)} %copy.105), calls=%async_computation.1 | async-start | bytes 1048576 | tf_op jit(solution)/shard_map/all_to_all | solution.py:99
  110.0 26.6 %copy-start.1 = (bf16[512,2,128,1]{0,2,3,1:T(8,128)(2,1)S(1)}, bf16[512,2,128,1]{0,2,3,1:T(8,128)(2,1)}, u32[]{:S(2)}) copy-start(bf16[512,2,128,1]{0,2,3,1:T(8,128)(2,1)} %copy.124) | copy-start | bytes 786436
  129.3 26.8 %all-to-all-start.2 = ((f32[128,6,8]{1,2,0:T(8,128)}), f32[128,6,8]{1,2,0:T(8,128)S(1)}, u32[]{:S(2)}, u32[]{:S(2)}) async-start(f32[128,6,8]{1,2,0:T(8,128)} %copy.112), calls=%async_computation.2 | async-start | bytes 1048576 | tf_op jit(solution)/shard_map/all_to_all | solution.py:106
  156.2 105.7 %all-to-all-start.3 = ((f32[128,6,1024]{2,1,0:T(8,128)}), f32[128,6,1024]{2,1,0:T(8,128)}, u32[]{:S(2)}, u32[]{:S(2)}) async-start(f32[128,6,1024]{2,1,0:T(8,128)} %reshape.214), calls=%async_computation.3 | async-start | bytes 8388608 | tf_op jit(solution)/shard_map/all_to_all | solution.py:92
  166.3 177.9 %all-gather.3.cloned.1.call-start = ((), (), s32[]{:S(2)}) async-start(), calls=%async_computation.4 | async-start | bytes 5242880 | tf_op jit(solution)/shard_map/all_gather | solution.py:130
  286.1 150.2 %all-gather.5.cloned.1.call-start = ((), (), s32[]{:S(2)}) async-start(), calls=%async_computation.5 | async-start | bytes 8454144 | tf_op jit(solution)/shard_map/all_gather | solution.py:133
Sparse Core Ops, SparseCore 0:
  286.2 57.9 all-gather.2
  347.3 88.9 all-gather.4
where the time goes:
time: 462 us; the launch traced here: 453 us
  waiting for transfers between devices  274 us (59%)
  local copies, waits for them, and re-layouts  55.6 us (12%)
  starting transfers between devices  44.6 us (10%)
  matrix products  38 us (8%)
  other arithmetic  27.1 us (6%)
  between operations  13.9 us (3%)
    all_gather x1, waiting for transfers between devices, on_device(): lax.all_gather(out_weight, 'seq', axis=0, tiled=True)  92.1 us
    all_to_all x1, waiting for transfers between devices, on_device(): lax.all_to_all(mixed_rows.reshape(sources, slot_width, features), 'seq',...  61.5 us
    all_gather x1, waiting for transfers between devices, on_device(): every_head = lax.all_gather(attention, 'head', axis=1, tiled=True)  57.3 us
    all_to_all x1, waiting for transfers between devices, on_device(): lax.all_to_all(outgoing, 'seq', split_axis=0, concat_axis=0, tiled=True)  47.6 us
    all_to_all x1, starting transfers between devices, on_device(): lax.all_to_all(outgoing, 'seq', split_axis=0, concat_axis=0, tiled=True)  18.4 us
    all_to_all x1, waiting for transfers between devices, on_device(): lax.all_to_all(jnp.transpose(peak_score, (2, 0, 1)).reshape(sources, slot...  11 us
    dot_general x1, matrix products, on_device(): jnp.dot(every_head, lax.all_gather(out_weight, 'seq', axis=0, tiled=True)...  10.1 us
    all_to_all x1, starting transfers between devices, on_device(): lax.all_to_all(mixed_rows.reshape(sources, slot_width, features), 'seq',...  10.1 us
  transfers between devices with their start and end apart: 6, of which 6 were waited for; matrix products, arithmetic and copies ran while one was open for 14% of the time, Pallas kernels for 0%

commit v1 on v0

--- a/solution.py
+++ b/solution.py
@@ -1,15 +1,262 @@
+import functools
 import math
 
 import jax
 import jax.numpy as jnp
 from jax import lax
+from jax.experimental import pallas as pl
+from jax.experimental.pallas import tpu as pltpu
 from jax.sharding import PartitionSpec as P
 
 HEAD_SIZE = 128
 CAP = 6
-
-
 NEG_FILL = -1e30
+MESH = pl.DeviceIdType.MESH
+
+
+def greet_all(owner_count):
+    me = lax.axis_index("seq")
+    barrier = pltpu.get_barrier_semaphore()
+
+    def greet(i, carry):
+        pl.semaphore_signal(
+            barrier, inc=1, device_id={"seq": lax.rem(me + i, owner_count)}, device_id_type=MESH
+        )
+        return carry
+
+    lax.fori_loop(1, owner_count, greet, 0)
+    pl.semaphore_wait(barrier, owner_count - 1)
+
+
+def down_kernel(owner_count, out_ref, in_ref, send_sem, recv_sem):
+    me = lax.axis_index("seq")
+    greet_all(owner_count)
+
+    def copy_to(b):
+        return pltpu.make_async_remote_copy(
+            src_ref=out_ref.at[b],
+            dst_ref=in_ref.at[me],
+            send_sem=send_sem.at[b],
+            recv_sem=recv_sem.at[me],
+            device_id={"seq": b},
+            device_id_type=MESH,
+        )
+
+    def copy_from(d):
+        return pltpu.make_async_remote_copy(
+            src_ref=out_ref.at[d],
+            dst_ref=in_ref.at[d],
+            send_sem=send_sem.at[d],
+            recv_sem=recv_sem.at[d],
+            device_id={"seq": d},
+            device_id_type=MESH,
+        )
+
+    lax.fori_loop(0, me, lambda i, c: (copy_to(me - 1 - i).start(), c)[1], 0)
+    lax.fori_loop(me + 1, owner_count, lambda d, c: (copy_from(d).wait_recv(), c)[1], 0)
+    lax.fori_loop(0, me, lambda b, c: (copy_to(b).wait_send(), c)[1], 0)
+
+
+def up_kernel(owner_count, out_ref, stat_out, in_ref, stat_in, send_sem, recv_sem):
+    me = lax.axis_index("seq")
+    greet_all(owner_count)
+
+    def copies(peer, slot):
+        return [
+            pltpu.make_async_remote_copy(
+                src_ref=source.at[peer],
+                dst_ref=target.at[slot],
+                send_sem=send_sem.at[k, peer],
+                recv_sem=recv_sem.at[k, slot],
+                device_id={"seq": peer},
+                device_id_type=MESH,
+            )
+            for k, (source, target) in enumerate(((out_ref, in_ref), (stat_out, stat_in)))
+        ]
+
+    def start(d, carry):
+        for copy in copies(d, me):
+            copy.start()
+        return carry
+
+    def wait_recv(b, carry):
+        for copy in copies(b, b):
+            copy.wait_recv()
+        return carry
+
+    def wait_send(d, carry):
+        for copy in copies(d, me):
+            copy.wait_send()
+        return carry
+
+    lax.fori_loop(me + 1, owner_count, start, 0)
+    lax.fori_loop(0, me, wait_recv, 0)
+    lax.fori_loop(me + 1, owner_count, wait_send, 0)
+
+
+def ring_steps(buf, axis_pos, extent, unit, to, sems):
+    up_send, up_recv, down_send, down_recv = sems
+    half = extent // 2
+
+    def up(step):
+        block = unit(lax.rem(axis_pos - step + 1 + extent, extent))
+        return pltpu.make_async_remote_copy(
+            src_ref=block, dst_ref=block, send_sem=up_send.at[step], recv_sem=up_recv.at[step],
+            device_id=to(lax.rem(axis_pos + 1, extent)), device_id_type=MESH)
+
+    def down(step):
+        block = unit(lax.rem(axis_pos + step - 1, extent))
+        return pltpu.make_async_remote_copy(
+            src_ref=block, dst_ref=block, send_sem=down_send.at[step], recv_sem=down_recv.at[step],
+            device_id=to(lax.rem(axis_pos + extent - 1, extent)), device_id_type=MESH)
+
+    return up, down, half
+
+
+def weight_kernel(w_ref, full, local_sem, send_sem, recv_sem, sib_send, sib_recv):
+    me = lax.axis_index("seq")
+    core = lax.rem(me, 2)
+    z = lax.rem(me // 2, 8)
+    y = me // 16
+
+    def at(yy, zz, cc):
+        return {"seq": (yy * 8 + zz) * 2 + cc}
+
+    barrier = pltpu.get_barrier_semaphore()
+    friends = [
+        at(y, lax.rem(z + 1, 8), core),
+        at(y, lax.rem(z + 7, 8), core),
+        at(lax.rem(y + 1, 8), z, core),
+        at(lax.rem(y + 7, 8), z, core),
+        at(y, z, 1 - core),
+    ]
+    for friend in friends:
+        pl.semaphore_signal(barrier, inc=1, device_id=friend, device_id_type=MESH)
+    local = pltpu.make_async_copy(w_ref, full.at[y, z, core], local_sem)
+    local.start()
+    pl.semaphore_wait(barrier, 5)
+    local.wait()
+
+    def rings(phase):
+        made = []
+        for h in range(2):
+            along_z = (h == 0) == (phase == 0)
+            sems = [s.at[phase, h, i] for i in range(2) for s in (send_sem, recv_sem)]
+            if along_z:
+                if phase == 0:
+                    unit = lambda p, h=h: full.at[y, p, core, h]
+                else:
+                    unit = lambda p, h=h: full.at[:, p, core, h]
+                made.append(ring_steps(full, z, 8, unit, lambda p: at(y, p, core), sems))
+            else:
+                if phase == 0:
+                    unit = lambda p, h=h: full.at[p, z, core, h]
+                else:
+                    unit = lambda p, h=h: full.at[p, :, core, h]
+                made.append(ring_steps(full, y, 8, unit, lambda p: at(p, z, core), sems))
+        return made
+
+    def sibling(h, p):
+        unit = full.at[p, :, core, h] if h == 0 else full.at[:, p, core, h]
+        return pltpu.make_async_remote_copy(
+            src_ref=unit, dst_ref=unit, send_sem=sib_send.at[h, p], recv_sem=sib_recv.at[h, p],
+            device_id=at(y, z, 1 - core), device_id_type=MESH)
+
+    def sibling_in(h, p):
+        unit = full.at[p, :, 1 - core, h] if h == 0 else full.at[:, p, 1 - core, h]
+        return pltpu.make_async_remote_copy(
+            src_ref=unit, dst_ref=unit, send_sem=sib_send.at[h, p], recv_sem=sib_recv.at[h, p],
+            device_id=at(y, z, 1 - core), device_id_type=MESH)
+
+    for phase in range(2):
+        made = rings(phase)
+        if phase == 1:
+            for h in range(2):
+                sibling(h, (y, z)[h]).start()
+        for step in range(1, 5):
+            for up, down, _ in made:
+                up(step).start()
+                if step < 4:
+                    down(step).start()
+            for h, (up, down, _) in enumerate(made):
+                pos = (y, z)[h]
+                up(step).wait_recv()
+                if phase == 1:
+                    sibling(h, lax.rem(pos - step + 8, 8)).start()
+                if step < 4:
+                    down(step).wait_recv()
+                    if phase == 1:
+                        sibling(h, lax.rem(pos + step, 8)).start()
+        for step in range(1, 5):
+            for up, down, _ in made:
+                up(step).wait_send()
+                if step < 4:
+                    down(step).wait_send()
+    for h in range(2):
+        for p in range(8):
+            sibling_in(h, p).wait_recv()
+            sibling(h, p).wait_send()
+
+
+def head_kernel(a_ref, full, local_sem, send_sem, recv_sem):
+    x = lax.axis_index("head")
+    right, left = lax.rem(x + 1, 4), lax.rem(x + 3, 4)
+    rows = a_ref.shape[0]
+    barrier = pltpu.get_barrier_semaphore()
+    for friend in (right, left):
+        pl.semaphore_signal(barrier, inc=1, device_id={"head": friend}, device_id_type=MESH)
+    local = pltpu.make_async_copy(a_ref, full.at[x], local_sem)
+    local.start()
+    pl.semaphore_wait(barrier, 2)
+
+    def move(k, src, dst, to):
+        return pltpu.make_async_remote_copy(
+            src_ref=src, dst_ref=dst, send_sem=send_sem.at[k], recv_sem=recv_sem.at[k],
+            device_id={"head": to}, device_id_type=MESH)
+
+    first = pl.ds(0, rows // 2)
+    second = pl.ds(rows // 2, rows // 2)
+    out = [
+        [move(0, a_ref.at[first], full.at[x, first], right), move(1, a_ref.at[second], full.at[x, second], right)],
+        [move(2, a_ref.at[second], full.at[x, second], left), move(3, a_ref.at[first], full.at[x, first], left)],
+    ]
+    for k in range(2):
+        for side in out:
+            side[k].start()
+    out[0][0].wait_recv()
+    onward = move(4, full.at[left, first], full.at[left, first], right)
+    onward.start()
+    out[1][0].wait_recv()
+    back = move(5, full.at[right, second], full.at[right, second], left)
+    back.start()
+    out[0][1].wait_recv()
+    out[1][1].wait_recv()
+    onward.wait_recv()
+    back.wait_recv()
+    for side in out:
+        for copy in side:
+            copy.wait_send()
+    onward.wait_send()
+    back.wait_send()
+    local.wait()
+
+
+VM = pl.BlockSpec(memory_space=pltpu.VMEM)
+DMA = pltpu.SemaphoreType.DMA
+
+
+def call(kernel, collective_id, out_shape, scratch, *args):
+    single = not isinstance(out_shape, (tuple, list))
+    return pl.pallas_call(
+        kernel,
+        out_shape=out_shape,
+        in_specs=[VM] * len(args),
+        out_specs=VM if single else [VM] * len(out_shape),
+        scratch_shapes=scratch,
+        compiler_params=pltpu.CompilerParams(
+            collective_id=collective_id, has_side_effects=True, vmem_limit_bytes=40 << 20
+        ),
+    )(*args)
 
 
 def own_partial(query_matrix, key_matrix, value_matrix, score_scale):
@@ -41,6 +288,7 @@
 def merge_parts(own_out, own_peak, own_total, pick_out, pick_peak, pick_total, live_rows):
     live_mask = live_rows[:, :, None]
     pick_peak = jnp.where(live_mask, pick_peak, own_peak[:, None, :])
+    pick_out = jnp.where(live_mask[..., None], pick_out, 0.0)
     summit = jnp.maximum(own_peak, jnp.max(pick_peak, axis=1))
     own_weight = own_total * jnp.exp(own_peak - summit)
     pick_weight = jnp.where(live_mask, pick_total * jnp.exp(pick_peak - summit[:, None, :]), 0.0)
@@ -58,6 +306,10 @@
     heads_per_group = heads_local // kv_local
     score_scale = 1.0 / math.sqrt(HEAD_SIZE)
     slot_count_total = owner_count * CAP
+    full_weight = call(
+        weight_kernel, 0, jax.ShapeDtypeStruct((8, 8, 2, 2, 16, 1024), jnp.bfloat16),
+        [DMA, DMA((2, 2, 2, 5)), DMA((2, 2, 2, 5)), DMA((2, 8)), DMA((2, 8))],
+        out_weight.reshape(2, 16, 1024))
     flat_picks = picks.reshape(-1)
     owner_ids = jnp.arange(owner_count, dtype=jnp.int32)
     matches = (flat_picks[:, None] == owner_ids[None, :]).astype(jnp.int32)
@@ -69,10 +321,16 @@
         .at[slot_index]
         .set(jnp.arange(2 * block_len, dtype=jnp.int32) // 2, mode="drop")
     )
-    outgoing = queries[slot_rows].reshape(owner_count, CAP, queries.shape[1])
+    outgoing = queries[slot_rows].reshape(owner_count, CAP * heads_local, HEAD_SIZE)
     key_heads = keys.reshape(block_len, kv_local, HEAD_SIZE)
     value_heads = values.reshape(block_len, kv_local, HEAD_SIZE)
-    arrived = lax.all_to_all(outgoing, "seq", split_axis=0, concat_axis=0, tiled=True)
+    arrived = call(
+        functools.partial(down_kernel, owner_count), 1,
+        jax.ShapeDtypeStruct(outgoing.shape, jnp.bfloat16),
+        [DMA((owner_count,)), DMA((owner_count,))], outgoing)
+    arrived = arrived.reshape(owner_count, CAP, heads_local * HEAD_SIZE)
+    live_source = jnp.arange(owner_count) > lax.axis_index("seq")
+    arrived = jnp.where(live_source[:, None, None], arrived, 0)
     sources, slot_width, features = arrived.shape
     query_matrix = arrived.reshape(sources * slot_width, kv_local, heads_per_group, HEAD_SIZE)
     scores = (
@@ -89,48 +347,42 @@
         preferred_element_type=jnp.float32,
     )
     mixed_rows = mixed_rows / jnp.transpose(totals, (2, 0, 1))[..., None]
-    part_out = lax.all_to_all(
-        mixed_rows.reshape(sources, slot_width, features),
-        "seq",
-        split_axis=0,
-        concat_axis=0,
-        tiled=True,
-    )
-    part_peak = lax.all_to_all(
-        jnp.transpose(peak_score, (2, 0, 1)).reshape(sources, slot_width, heads_local),
-        "seq",
-        split_axis=0,
-        concat_axis=0,
-        tiled=True,
-    )
-    part_total = lax.all_to_all(
-        jnp.transpose(totals, (2, 0, 1)).reshape(sources, slot_width, heads_local),
-        "seq",
-        split_axis=0,
-        concat_axis=0,
-        tiled=True,
-    )
+    part_out = mixed_rows.astype(jnp.bfloat16).reshape(sources, slot_width * heads_local, HEAD_SIZE)
+    stats = jnp.concatenate(
+        [
+            jnp.transpose(peak_score, (2, 0, 1)).reshape(sources, slot_width * heads_local),
+            jnp.transpose(totals, (2, 0, 1)).reshape(sources, slot_width * heads_local),
+        ],
+        axis=1,
+    )
+    stats = jnp.pad(stats, ((0, 0), (0, 128 - stats.shape[1])))[:, None, :]
+    part_out, stats = call(
+        functools.partial(up_kernel, owner_count), 2,
+        [jax.ShapeDtypeStruct(part_out.shape, jnp.bfloat16), jax.ShapeDtypeStruct(stats.shape, jnp.float32)],
+        [DMA((2, owner_count)), DMA((2, owner_count))], part_out, stats)
+    count = slot_width * heads_local
+    part_peak = stats[:, 0, :count].reshape(slot_count_total, heads_local)
+    part_total = stats[:, 0, count:2 * count].reshape(slot_count_total, heads_local)
     safe_index = jnp.minimum(slot_index, slot_count_total - 1)
     pick_out = part_out.reshape(slot_count_total, heads_local, HEAD_SIZE)[safe_index].reshape(
         block_len, 2, heads_local, HEAD_SIZE
     )
-    pick_peak = part_peak.reshape(slot_count_total, heads_local)[safe_index].reshape(
-        block_len, 2, heads_local
-    )
-    pick_total = part_total.reshape(slot_count_total, heads_local)[safe_index].reshape(
-        block_len, 2, heads_local
-    )
+    pick_peak = part_peak[safe_index].reshape(block_len, 2, heads_local)
+    pick_total = part_total[safe_index].reshape(block_len, 2, heads_local)
     live_rows = is_live.reshape(block_len, 2)
     local_rows = queries.reshape(block_len, kv_local, heads_per_group, HEAD_SIZE)
     own_out, own_peak, own_total = own_partial(local_rows, key_heads, value_heads, score_scale)
     attention = merge_parts(
-        own_out, own_peak, own_total, pick_out, pick_peak, pick_total, live_rows
+        own_out, own_peak, own_total, pick_out.astype(jnp.float32), pick_peak, pick_total, live_rows
     )
     attention = attention.reshape(block_len, heads_local * HEAD_SIZE).astype(jnp.bfloat16)
-    every_head = lax.all_gather(attention, "head", axis=1, tiled=True)
-    return jnp.dot(
+    every_head = call(
+        head_kernel, 3, jax.ShapeDtypeStruct((4, block_len, heads_local * HEAD_SIZE), jnp.bfloat16),
+        [DMA, DMA((6,)), DMA((6,))], attention)
+    return jnp.einsum(
+        "hti,hio->to",
         every_head,
-        lax.all_gather(out_weight, "seq", axis=0, tiled=True),
+        full_weight.reshape(4, 1024, 1024),
         preferred_element_type=jnp.float32,
     ).astype(jnp.bfloat16)
 

time: 462 us -> 315 us (0.68)
  the two profiles are of different devices: /device:TPU:1 before, /device:TPU:56 now
where the time goes in v1:
time: 315 us; the launch traced here: 311 us
  Pallas kernels  215 us (68%)
  local copies, waits for them, and re-layouts  44.5 us (14%)
  other arithmetic  26 us (8%)
  matrix products  24.8 us (8%)
    pallas_call x4, Pallas kernels, call(): pl.pallas_call(kernel, out_shape=out_shape, in_specs=[VM] * len(args), ou...  215 us
    gather x1, local copies, waits for them, and re-layouts, on_device(): part_out.reshape(slot_count_total, heads_local, HEAD_SIZE)[safe_index]  7.59 us
    dot_general x1, matrix products, own_partial(): jnp.einsum('jgqk,kjd->qjgd', weights.astype(jnp.bfloat16), value_matrix,...  7.21 us

profile of v1, /device:TPU:56, one launch (start us, length us, event | category | flops | bytes accessed | tf_op | source)
XLA Modules:
  0.0 310.6 jit_solution(12692061982763613437)
XLA Ops:
  0.0 1.1 reshape.216
  1.1 0.9 copy.127
  2.0 1.0 reshape.209
  3.0 0.7 broadcast_compare_fusion
  3.7 0.2 copy.98
  3.9 0.2 ge.22
  4.1 0.7 broadcast_multiply_fusion
  5.0 0.2 mul.82
  5.2 0.8 copy.101
  6.0 0.2 eq.29
  6.3 0.2 fusion.27
  6.7 0.2 eq.25
  6.8 0.4 fusion.26
  7.2 4.3 %scatter_custom_fusion = s32[768]{0:T(1024)S(1)} fusion(s32[1024]{0:T(1024)S(1)} %bitcast.111, s32[1024]{0:T(1024)S(1)} %add_select_fusion, s32[]{:T(128)} %constant.42.clone.1), kind=kCustom, calls=%fused_computation.71 | custom fusion | bytes 3076 | tf_op jit(solution)/shard_map/scatter | solution.py:322
  11.6 3.6 %gather_fusion = bf16[768,1024]{1,0:T(8,128)(2,1)} fusion(bf16[512,1024]{1,0:T(8,128)(2,1)S(1)} %copy-done.1, s32[1024]{0:T(1024)S(1)} %pad_clamp_fusion), kind=kCustom, calls=%fused_computation | custom fusion | bytes 3148800 | tf_op jit(solution)/shard_map/gather | solution.py:324
  15.2 2.5 reshape.214.out_ref
  17.7 54.0 %shard_map.55 = bf16[128,48,128]{2,1,0:T(8,128)(2,1)S(1)} custom-call(bf16[128,48,128]{2,1,0:T(8,128)(2,1)S(1)} %reshape.214.out_ref), custom_call_target="tpu_custom_call" | custom-call | tf_op jit(solution)/shard_map/pallas_call | solution.py:250
  71.9 0.2 broadcast_in_dim.99
  72.0 1.9 bitcast_reduce_fusion
  74.0 2.1 fusion.1
  76.1 4.0 %fusion.15 = bf16[768,2,4,128]{3,0,2,1:T(8,128)(2,1)S(1)} fusion(bf16[512,2,128,1]{0,2,3,1:T(8,128)(2,1)S(1)} %copy-done.9, f32[2,768,4,512]{1,3,2,0:T(8,128)S(1)} %get-tuple-element.18, f32[2,4,768]{2,1,0:T(4,128)S(1)} %get-tuple-element.17, f32[768,2,4]{0,2,1:T(4,128)S(1)} %bitcast.104), kind=kOutput, calls=%fused_computation.24 | convolution fusion | flops 816316416 | bytes 14467072 | tf_op jit(solution)/shard_map/jgsk,kjd->sjgd/dot_general | solution.py:343
  80.1 1.2 copy.109
  81.4 0.5 copy.111
  81.8 0.6 reshape.219
  82.4 0.5 copy.110
  82.9 0.6 reshape.218
  83.6 72.4 %shard_map.56 = (bf16[128,48,128]{2,1,0:T(8,128)(2,1)S(1)}, f32[128,1,128]{2,1,0:T(1,128)S(1)}) custom-call(bf16[128,48,128]{2,1,0:T(8,128)(2,1)S(1)} %bitcast.88, f32[128,1,128]{2,1,0:T(1,128)S(1)} %bitcast.91), custom_call_target="tpu_custom_call" | custom-call | tf_op jit(solution)/shard_map/pallas_call | solution.py:250
  156.0 0.4 slice_reduce_fusion
  156.6 3.0 gather_fusion.2
  159.8 2.7 reshape.210
  162.5 6.1 %fusion.3 = (f32[2,4,512]{2,1,0:T(4,128)S(1)}, f32[2,512,512,4]{2,1,3,0:T(8,128)}) fusion(pred[512,512]{0,1:T(8,128)(4,1)S(1)} %iota_compare_fusion, bf16[512,2,4,128]{3,2,1,0:T(4,128)(2,1)} %reshape.210, bf16[512,2,128,1]{2,1,0,3:T(2,128)(2,1)S(1)} %bitcast.101), kind=kOutput, calls=%fused_computation.12 | convolution fusion | flops 543158272 | bytes 9977856 | tf_op jit(solution)/shard_map/qjgd,kjd->jgqk/dot_general | solution.py:266
  168.6 0.6 copy-done.11
  169.3 2.8 gather_fusion.1
  172.3 3.4 %fusion.29 = f32[512,8]{1,0:T(8,128)S(1)} fusion(f32[512,2,8]{2,1,0:T(2,128)S(1)} %bitcast.96, pred[512,2]{1,0:T(8,128)(4,1)S(1)} %copy-done.3, f32[512,8]{1,0:T(8,128)S(1)} %copy.112), kind=kLoop, calls=%fused_computation.47 | loop fusion | flops 12288 | bytes 66560 | tf_op jit(solution)/shard_map/reduce_max | solution.py:292
  175.8 0.9 copy.118
  176.6 4.6 %fusion.44 = (f32[512,8]{1,0:T(8,128)}, f32[512,2,8]{2,1,0:T(2,128)S(1)}) fusion(f32[512,2,8]{2,1,0:T(2,128)S(1)} %bitcast.99, f32[512,8]{1,0:T(8,128)} %copy.118, f32[512,2,8]{2,1,0:T(2,128)S(1)} %bitcast.97, f32[512,8]{1,0:T(8,128)S(1)} %copy.112, pred[512,2]{1,0:T(8,128)(4,1)} %copy-done.2), kind=kLoop, calls=%fused_computation.81 | loop fusion | flops 36864 | bytes 148480 | tf_op jit(solution)/shard_map/reduce_sum | solution.py:298
  181.2 1.0 copy.120
  182.3 4.5 %fusion.9 = f32[2,4,512]{2,1,0:T(4,128)S(1)} fusion(f32[2,512,512,4]{2,1,3,0:T(8,128)} %get-tuple-element.20, f32[2,4,512]{2,1,0:T(4,128)S(1)} %copy-done.12, pred[512,512]{0,1:T(8,128)(4,1)} %copy-done.7), kind=kLoop, calls=%fused_computation.17 | loop fusion | flops 10481664 | bytes 8683520 | tf_op jit(solution)/shard_map/reduce_sum | solution.py:273
  187.0 2.0 div.38
  189.0 7.6 %gather_fusion.3 = bf16[1024,8,128]{2,1,0:T(8,128)(2,1)} fusion(bf16[768,8,128]{2,1,0:T(8,128)(2,1)S(1)} %bitcast.90, s32[1024]{0:T(1024)S(1)} %copy-done.15), kind=kCustom, calls=%fused_computation.3 | custom fusion | bytes 4198400 | tf_op jit(solution)/shard_map/gather | solution.py:367
  196.6 5.7 %fusion.11 = f32[512,8,128]{2,1,0:T(8,128)S(1)} fusion(f32[512,2,8]{2,1,0:T(2,128)S(1)} %get-tuple-element.14, pred[512,2]{1,0:T(8,128)(4,1)S(1)} %copy-done.4, bf16[1024,8,128]{2,1,0:T(8,128)(2,1)} %gather_fusion.3), kind=kLoop, calls=%fused_computation.20 | loop fusion | flops 3670016 | bytes 4228096 | tf_op jit(solution)/shard_map/reduce_sum | solution.py:295
  202.3 7.2 %bitcast_divide_fusion.2 = f32[512,2,4,128]{0,3,2,1:T(8,128)} fusion(bf16[512,2,128,1]{0,2,3,1:T(8,128)(2,1)S(1)} %copy-done.10, f32[2,512,512,4]{2,1,3,0:T(8,128)} %get-tuple-element.20, f32[2,4,512]{2,1,0:T(4,128)S(1)} %copy-done.13, pred[512,512]{0,1:T(8,128)(4,1)S(1)} %copy-done.8, f32[512,2,4]{0,2,1:T(4,128)S(1)} %bitcast.108), kind=kOutput, calls=%fused_computation.30 | convolution fusion | flops 547880960 | bytes 11042816 | tf_op jit(solution)/shard_map/jgqk,kjd->qjgd/dot_general | solution.py:274
  209.6 2.9 copy.136
  212.6 0.6 mul.88
  213.2 3.4 %fusion.16.a_ref = bf16[512,1024]{1,0:T(8,128)(2,1)S(1)} fusion(f32[64,8,8,128]{3,2,1,0:T(8,128)} %bitcast.94, f32[64,8,8,128]{3,2,1,0:T(8,128)S(1)} %bitcast.93, f32[512,1024]{1,0:T(8,128)} %copy.136, f32[64,8,8,128]{3,2,1,0:T(8,128)S(1)} %bitcast.95), kind=kLoop, calls=%fused_computation.26 | loop fusion | flops 2097152 | bytes 9437184 | tf_op jit(solution)/shard_map/convert_element_type | solution.py:378
  216.6 38.7 %shard_map.57 = bf16[4,512,1024]{2,1,0:T(8,128)(2,1)S(1)} custom-call(bf16[512,1024]{1,0:T(8,128)(2,1)S(1)} %fusion.16.a_ref), custom_call_target="tpu_custom_call" | custom-call | tf_op jit(solution)/shard_map/pallas_call | solution.py:250
  255.3 49.8 %shard_map.58 = bf16[8,8,2,2,16,1024]{5,4,3,2,1,0:T(8,128)(2,1)S(1)} custom-call(bf16[2,16,1024]{2,1,0:T(8,128)(2,1)S(1)} %bitcast.92), custom_call_target="tpu_custom_call" | custom-call | tf_op jit(solution)/shard_map/pallas_call | solution.py:250
  305.1 5.5 %bitcast_convert_fusion = bf16[512,1024]{1,0:T(8,128)(2,1)} fusion(bf16[4,512,1024]{2,1,0:T(8,128)(2,1)S(1)} %shard_map.57, bf16[4,1024,1024]{2,1,0:T(8,128)(2,1)S(1)} %bitcast.87), kind=kOutput, calls=%fused_computation.29 | convolution fusion | flops 4295491584 | bytes 13631488 | tf_op jit(solution)/shard_map/hti,hio->to/dot_general | solution.py:382
  (57 shorter events, 1.6 us)
Async XLA Ops:
  0.0 11.6 %copy-start.1 = (bf16[512,1024]{1,0:T(8,128)(2,1)S(1)}, bf16[512,1024]{1,0:T(8,128)(2,1)}, u32[]{:S(2)}) copy-start(bf16[512,1024]{1,0:T(8,128)(2,1)} %param.5) | copy-start | bytes 3145732
  3.0 69.0 %copy-start.5 = (bf16[512,2,128]{2,1,0:T(2,128)(2,1)}, bf16[512,2,128]{2,1,0:T(2,128)(2,1)S(1)}, u32[]{:S(2)}) copy-start(bf16[512,2,128]{2,1,0:T(2,128)(2,1)S(1)} %reshape.209) | copy-start | bytes 786436
  3.9 1.0 copy-start.2
  74.0 2.1 copy-start.9
  156.0 6.4 %copy-start.6 = (bf16[512,2,128]{2,1,0:T(2,128)(2,1)S(1)}, bf16[512,2,128]{2,1,0:T(2,128)(2,1)}, u32[]{:S(2)}) copy-start(bf16[512,2,128]{2,1,0:T(2,128)(2,1)} %copy-done.5) | copy-start | bytes 786436
  156.6 12.7 %copy-start.14 = (s32[1024]{0:T(1024)}, s32[1024]{0:T(1024)S(1)}, u32[]{:S(2)}) copy-start(s32[1024]{0:T(1024)S(1)} %broadcast_clamp_fusion) | copy-start | bytes 12292
  159.8 8.8 %copy-start.7 = (pred[512,512]{0,1:T(8,128)(4,1)}, pred[512,512]{0,1:T(8,128)(4,1)S(1)}, u32[]{:S(2)}) copy-start(pred[512,512]{0,1:T(8,128)(4,1)S(1)} %iota_compare_fusion) | copy-start | bytes 786436
  168.6 0.6 copy-start.11
  168.6 3.7 %copy-start.3 = (pred[512,2]{1,0:T(8,128)(4,1)S(1)}, pred[512,2]{1,0:T(8,128)(4,1)}, u32[]{:S(2)}) copy-start(pred[512,2]{1,0:T(8,128)(4,1)} %copy-done.2) | copy-start | bytes 3076
  172.2 10.1 %copy-start.12 = (f32[2,4,512]{2,1,0:T(4,128)S(1)}, f32[2,4,512]{2,1,0:T(4,128)}, u32[]{:S(2)}) copy-start(f32[2,4,512]{2,1,0:T(4,128)} %copy-done.11) | copy-start | bytes 49156
  182.3 6.7 %copy-start.15 = (s32[1024]{0:T(1024)S(1)}, s32[1024]{0:T(1024)}, u32[]{:S(2)}) copy-start(s32[1024]{0:T(1024)} %copy-done.14) | copy-start | bytes 12292
  186.8 9.8 %copy-start.4 = (pred[512,2]{1,0:T(8,128)(4,1)S(1)}, pred[512,2]{1,0:T(8,128)(4,1)}, u32[]{:S(2)}) copy-start(pred[512,2]{1,0:T(8,128)(4,1)} %copy-done.2) | copy-start | bytes 3076
  189.0 13.3 %copy-start.8 = (pred[512,512]{0,1:T(8,128)(4,1)S(1)}, pred[512,512]{0,1:T(8,128)(4,1)}, u32[]{:S(2)}) copy-start(pred[512,512]{0,1:T(8,128)(4,1)} %copy-done.7) | copy-start | bytes 786436
  189.0 13.3 %copy-start.10 = (bf16[512,2,128,1]{0,2,3,1:T(8,128)(2,1)S(1)}, bf16[512,2,128,1]{0,2,3,1:T(8,128)(2,1)}, u32[]{:S(2)}) copy-start(bf16[512,2,128,1]{0,2,3,1:T(8,128)(2,1)} %copy.127) | copy-start | bytes 786436
  189.0 13.3 %copy-start.13 = (f32[2,4,512]{2,1,0:T(4,128)S(1)}, f32[2,4,512]{2,1,0:T(4,128)}, u32[]{:S(2)}) copy-start(f32[2,4,512]{2,1,0:T(4,128)} %copy-done.11) | copy-start | bytes 49156
  216.6 38.7 %copy-start = (bf16[32,1024]{1,0:T(8,128)(2,1)S(1)}, bf16[32,1024]{1,0:T(8,128)(2,1)}, u32[]{:S(2)}) copy-start(bf16[32,1024]{1,0:T(8,128)(2,1)} %param.9) | copy-start | bytes 196612

commit v2 on v0

v2 whole, which is shorter than its diff:
```python
import functools
import math

import jax
import jax.numpy as jnp
from jax import lax
from jax.experimental import pallas as pl
from jax.experimental.pallas import tpu as pltpu
from jax.sharding import PartitionSpec as P

HEAD = 128
CAP = 6
BLOCK = 512
OWNERS = 128
GROUP = 4
KV = 2
ROWS = CAP * GROUP
SLOTS = CAP * OWNERS
BATCH = 8
MESH = pl.DeviceIdType.MESH
F32 = jnp.float32
BF16 = jnp.bfloat16
LOG2E = 1.0 / math.log(2.0)
SCALE = LOG2E / math.sqrt(HEAD)


def dot(a, b):
    return lax.dot_general(a, b, (((1,), (0,)), ((), ())), preferred_element_type=F32)


def dot_t(a, b):
    return lax.dot_general(a, b, (((1,), (1,)), ((), ())), preferred_element_type=F32)


def loop(low, high, body):
    def step(i, carry):
        body(i)
        return carry

    lax.fori_loop(low, high, step, 0)


def iota(shape, dim):
    return lax.broadcasted_iota(jnp.int32, shape, dim)


def kernel(
    q_ref, k_ref, v_ref, picks_ref, w_ref, out_ref,
    rows32, q_out, q_in, part_out, part_in, stat_out, stat_in,
    own_out, own_peak, own_total, pick_rank, choose, full, every, total,
    q_send, q_recv, p_send, p_recv, s_send, s_recv,
    w_local, w_send, w_recv, sib_send, sib_recv, x_send, x_recv,
):
    me = lax.axis_index("seq")
    x = lax.axis_index("head")
    core = lax.rem(me, 2)
    z = lax.rem(me // 2, 8)
    y = me // 16
    right, left = lax.rem(x + 1, 4), lax.rem(x + 3, 4)

    part_in[...] = jnp.zeros_like(part_in)
    stat_in[...] = jnp.zeros_like(stat_in)

    barrier = pltpu.get_barrier_semaphore()
    loop(1, OWNERS, lambda i: pl.semaphore_signal(
        barrier, inc=1, device_id={"seq": lax.rem(me + i, OWNERS)}, device_id_type=MESH))
    for friend in (right, left):
        pl.semaphore_signal(barrier, inc=1, device_id={"head": friend}, device_id_type=MESH)

    w_copy = pltpu.make_async_copy(w_ref, full.at[y, z, core], w_local)
    w_copy.start()

    picks = picks_ref[...]
    first, second = picks[:, 0:1], picks[:, 1:2]
    lanes = iota((BLOCK, OWNERS), 1)
    hit0, hit1 = first == lanes, second == lanes
    named = jnp.where(hit0 | hit1, 1.0, 0.0).astype(BF16)
    before = jnp.where(iota((BLOCK, BLOCK), 0) > iota((BLOCK, BLOCK), 1), 1.0, 0.0).astype(BF16)
    rank = dot(before, named)
    rank0 = jnp.sum(jnp.where(hit0, rank, 0.0), axis=1, keepdims=True).astype(jnp.int32)
    rank1 = jnp.sum(jnp.where(hit1, rank, 0.0), axis=1, keepdims=True).astype(jnp.int32)
    pick_rank[0] = rank0
    pick_rank[1] = rank1
    slot0 = jnp.where(first >= 0, rank0 * OWNERS + first, -1)
    slot1 = jnp.where(second >= 0, rank1 * OWNERS + second, -1)
    for r in range(CAP):
        at = iota((BLOCK, OWNERS), 1) + r * OWNERS
        choose[0:BLOCK, r * OWNERS:(r + 1) * OWNERS] = jnp.where(slot0 == at, 1.0, 0.0).astype(BF16)
        choose[BLOCK:, r * OWNERS:(r + 1) * OWNERS] = jnp.where(slot1 == at, 1.0, 0.0).astype(BF16)
    slots = jnp.where(lanes == 0, slot0, jnp.where(lanes == 1, slot1, -1)).astype(F32)
    slots = jnp.transpose(slots)
    across0, across1 = slots[0:1].astype(jnp.int32), slots[1:2].astype(jnp.int32)
    for r in range(CAP):
        at = iota((OWNERS, BLOCK), 0) + r * OWNERS
        pick = jnp.where((across0 == at) | (across1 == at), 1.0, 0.0).astype(BF16)
        for j in range(KV):
            got = dot(pick, q_ref[:, j * GROUP * HEAD:(j + 1) * GROUP * HEAD])
            for g in range(GROUP):
                rows32[j, pl.ds(GROUP * r + g, OWNERS, ROWS), :] = got[:, g * HEAD:(g + 1) * HEAD]

    def pack(j):
        def some(i):
            block = rows32[j, pl.ds(pl.multiple_of(i * 16 * ROWS, 16 * ROWS), 16 * ROWS), :]
            q_out[j, pl.ds(i * 16, 16)] = block.reshape(16, ROWS, HEAD).astype(BF16)

        loop(0, OWNERS // 16, some)

    for j in range(KV):
        pack(j)
    w_copy.wait()
    pl.semaphore_wait(barrier, OWNERS + 1)

    def move(src, dst, send_sem, recv_sem, to):
        return pltpu.make_async_remote_copy(
            src_ref=src, dst_ref=dst, send_sem=send_sem, recv_sem=recv_sem,
            device_id=to, device_id_type=MESH)

    def query(j, peer, slot):
        return move(q_out.at[j, peer], q_in.at[j, slot], q_send.at[j, peer], q_recv.at[j, slot], {"seq": peer})

    def part(j, peer, slot):
        return move(part_out.at[j, peer], part_in.at[j, slot], p_send.at[j, peer], p_recv.at[j, slot], {"seq": peer})

    def stat(j, peer, slot):
        return move(stat_out.at[j, peer], stat_in.at[j, slot], s_send.at[j, peer], s_recv.at[j, slot], {"seq": peer})

    def send_queries(j):
        loop(0, me, lambda i: query(j, me - 1 - i, me).start())

    def device(yy, zz, cc):
        return {"seq": (yy * 8 + zz) * 2 + cc}

    def w_unit(phase, h, p, c):
        if phase == 0:
            return full.at[y, p, c, h] if h == 0 else full.at[p, z, c, h]
        return full.at[p, :, c, h] if h == 0 else full.at[:, p, c, h]

    def w_move(phase, h, step, way):
        along_z = (h == 0) == (phase == 0)
        pos = z if along_z else y
        ahead = lax.rem(pos + 8 + way, 8)
        unit = w_unit(phase, h, lax.rem(pos - way * (step - 1) + 8, 8), core)
        to = device(y, ahead, core) if along_z else device(ahead, z, core)
        i = 0 if way > 0 else 1
        return move(unit, unit, w_send.at[phase, h, i, step], w_recv.at[phase, h, i, step], to)

    def sibling(h, p, c):
        unit = w_unit(1, h, p, c)
        return move(unit, unit, sib_send.at[h, p], sib_recv.at[h, p], device(y, z, 1 - core))

    def w_moves(phase, step):
        ways = (1, -1) if step < 4 else (1,)
        return [(h, way, w_move(phase, h, step, way)) for way in ways for h in range(2)]

    def w_start(phase, step):
        if phase == 1 and step == 1:
            for h in range(2):
                sibling(h, (y, z)[h], core).start()
        for _, _, copy in w_moves(phase, step):
            copy.start()

    def w_wait(phase, step):
        for h, way, copy in w_moves(phase, step):
            copy.wait_recv()
            if phase == 1:
                sibling(h, lax.rem((y, z)[h] - way * step + 8, 8), core).start()

    def w_next(phase, step):
        w_wait(phase, step)
        if step < 4:
            w_start(phase, step + 1)
        elif phase == 0:
            w_start(1, 1)

    def own(h):
        j = h // GROUP
        for part_no in range(2):
            rows = slice(part_no * 256, part_no * 256 + 256)
            keys = (part_no + 1) * 256
            s = dot_t(q_ref[rows, h * HEAD:(h + 1) * HEAD], k_ref[0:keys, j * HEAD:(j + 1) * HEAD])
            seen = iota((256, keys), 1) <= iota((256, keys), 0) + part_no * 256
            s = jnp.where(seen, s, -1e30)
            peak = jnp.max(s, axis=1, keepdims=True)
            weights = jnp.exp2((s - peak) * SCALE)
            own_peak[h, rows] = peak * SCALE
            own_total[h, rows] = jnp.sum(weights, axis=1, keepdims=True)
            own_out[rows, h * HEAD:(h + 1) * HEAD] = dot(
                weights.astype(BF16), v_ref[0:keys, j * HEAD:(j + 1) * HEAD])

    def remote(j, n):
        base = n * BATCH
        low = jnp.maximum(base, me + 1)
        loop(low, base + BATCH, lambda d: query(j, d, d).wait_recv())
        batch = pl.ds(base, BATCH)
        rows = q_in[j, batch].astype(F32).reshape(BATCH * ROWS, HEAD).astype(BF16)
        s = dot_t(rows, k_ref[:, j * HEAD:(j + 1) * HEAD])
        peak = jnp.max(s, axis=1, keepdims=True)
        weights = jnp.exp2((s - peak) * SCALE)
        mass = jnp.sum(weights, axis=1, keepdims=True)
        mixed = dot(weights.astype(BF16), v_ref[:, j * HEAD:(j + 1) * HEAD]) * (1.0 / mass)
        part_out[j, batch] = mixed.reshape(BATCH, ROWS, HEAD).astype(BF16)
        level = peak * SCALE + jnp.log(mass) * LOG2E
        level = jnp.broadcast_to(level, (BATCH * ROWS, HEAD)).reshape(BATCH, ROWS, HEAD)
        diagonal = iota(level.shape, 1) == iota(level.shape, 2)
        stat_out[j, batch] = jnp.sum(jnp.where(diagonal, level, 0.0), axis=1, keepdims=True)

        def answer(d):
            part(j, d, me).start()
            stat(j, d, me).start()

        loop(low, base + BATCH, answer)

    low_batch = (me + 1) // BATCH
    batches = OWNERS // BATCH - low_batch

    def remote_some(j, i, count):
        loop(low_batch + batches * i // count, low_batch + batches * (i + 1) // count, lambda n: remote(j, n))

    def combine(j):
        def arrived(b):
            part(j, b, b).wait_recv()
            stat(j, b, b).wait_recv()

        loop(0, me, arrived)

        def widen(i):
            rows32[j, pl.ds(pl.multiple_of(i * 16 * ROWS, 16 * ROWS), 16 * ROWS), :] = (
                part_in[j, pl.ds(i * 16, 16)].astype(F32).reshape(16 * ROWS, HEAD))

        loop(0, OWNERS // 16, widen)
        picks = picks_ref[...]
        lane = iota((BLOCK, OWNERS), 1)
        levels = jnp.sum(stat_in[j], axis=1)
        high = levels.astype(BF16)
        rest = levels - high.astype(F32)
        mid = rest.astype(BF16)
        low = (rest - mid.astype(F32)).astype(BF16)
        found = []
        for c in range(2):
            hit = jnp.where(picks[:, c:c + 1] == lane, 1.0, 0.0).astype(BF16)
            found.append(dot(hit, high) + dot(hit, mid) + dot(hit, low))
        for g in range(GROUP):
            h = j * GROUP + g
            source = jnp.concatenate(
                [rows32[j, pl.ds(GROUP * r + g, OWNERS, ROWS), :].astype(BF16) for r in range(CAP)], axis=0)
            got = dot(choose[...], source)
            peak, mass = own_peak[h], own_total[h]
            level, live = [], []
            for c in range(2):
                here = lane == pick_rank[c] * GROUP + g
                live.append(picks[:, c:c + 1] >= 0)
                level.append(jnp.sum(jnp.where(here, found[c], 0.0), axis=1, keepdims=True))
            top = peak
            for c in range(2):
                top = jnp.maximum(top, jnp.where(live[c], level[c], peak))
            own_share = jnp.exp2(peak - top)
            share = [jnp.where(live[c], jnp.exp2(level[c] - top), 0.0) for c in range(2)]
            norm = 1.0 / (own_share * mass + share[0] + share[1])
            mixed = own_out[:, h * HEAD:(h + 1) * HEAD] * (own_share * norm)
            mixed += got[0:BLOCK] * (share[0] * norm) + got[BLOCK:] * (share[1] * norm)
            every[x, j, :, g * HEAD:(g + 1) * HEAD] = mixed.astype(BF16)

    upper, lower = pl.ds(0, BLOCK // 2), pl.ds(BLOCK // 2, BLOCK // 2)

    def x_move(j, i, owner, rows, to):
        unit = every.at[owner, j, rows]
        return move(unit, unit, x_send.at[j, i], x_recv.at[j, i], {"head": to})

    def x_copies(j):
        return [
            x_move(j, 0, x, upper, right), x_move(j, 1, x, lower, left),
            x_move(j, 2, x, lower, right), x_move(j, 3, x, upper, left),
        ]

    def x_onward(j):
        return [x_move(j, 4, left, upper, right), x_move(j, 5, right, lower, left)]

    def x_start(j):
        for copy in x_copies(j):
            copy.start()

    def x_forward(j):
        copies, onward = x_copies(j), x_onward(j)
        for i in range(2):
            copies[i].wait_recv()
            onward[i].start()

    def project(owner, j, first_term):
        a = every[owner, j]
        for n in range(4):
            cols = slice(n * 256, n * 256 + 256)
            w = full[2 * owner + j, :, :, :, :, cols].reshape(BLOCK, 256)
            term = dot(a, w)
            total[:, cols] = term if first_term else total[:, cols] + term

    send_queries(0)
    w_start(0, 1)
    own(0)
    send_queries(1)
    for h in range(1, KV * GROUP):
        own(h)
        if h % 2 == 1:
            w_next(0, h // 2 + 1)
    remote_some(0, 0, 2)
    w_next(1, 1)
    remote_some(0, 1, 2)
    w_next(1, 2)
    remote_some(1, 0, 2)
    combine(0)
    x_start(0)
    w_next(1, 3)
    remote_some(1, 1, 2)
    x_forward(0)
    w_wait(1, 4)
    combine(1)
    x_start(1)

    def w_sent(phase):
        for step in range(1, 5):
            for _, _, copy in w_moves(phase, step):
                copy.wait_send()

    for phase in range(2):
        w_sent(phase)
    for h in range(2):
        for p in range(8):
            sibling(h, p, 1 - core).wait_recv()
            sibling(h, p, core).wait_send()
    for copy in x_copies(0)[2:] + x_onward(0):
        copy.wait_recv()
    project(x, 0, True)
    project(left, 0, False)
    project(right, 0, False)
    x_forward(1)
    project(lax.rem(x + 2, 4), 0, False)
    project(x, 1, False)

    def sent_queries(b):
        for j in range(KV):
            query(j, b, me).wait_send()

    def sent_parts(d):
        for j in range(KV):
            part(j, d, me).wait_send()
            stat(j, d, me).wait_send()

    loop(0, me, sent_queries)
    loop(me + 1, OWNERS, sent_parts)
    for copy in x_copies(1)[2:]:
        copy.wait_recv()
    project(left, 1, False)
    project(right, 1, False)
    for copy in x_onward(1):
        copy.wait_recv()
    project(lax.rem(x + 2, 4), 1, False)
    out_ref[...] = total[...].astype(BF16)
    for j in range(KV):
        for copy in x_copies(j) + x_onward(j):
            copy.wait_send()


def on_device(queries, keys, values, picks, out_weight):
    vmem, dma = pltpu.VMEM, pltpu.SemaphoreType.DMA
    features = out_weight.shape[1]
    return pl.pallas_call(
        kernel,
        out_shape=jax.ShapeDtypeStruct((BLOCK, features), BF16),
        in_specs=[pl.BlockSpec(memory_space=vmem)] * 5,
        out_specs=pl.BlockSpec(memory_space=vmem),
        scratch_shapes=[
            vmem((KV, OWNERS * ROWS, HEAD), F32),
            vmem((KV, OWNERS, ROWS, HEAD), BF16),
            vmem((KV, OWNERS, ROWS, HEAD), BF16),
            vmem((KV, OWNERS, ROWS, HEAD), BF16),
            vmem((KV, OWNERS, ROWS, HEAD), BF16),
            vmem((KV, OWNERS, 1, HEAD), F32),
            vmem((KV, OWNERS, 1, HEAD), F32),
            vmem((BLOCK, KV * GROUP * HEAD), F32),
            vmem((KV * GROUP, BLOCK, 1), F32),
            vmem((KV * GROUP, BLOCK, 1), F32),
            vmem((2, BLOCK, 1), jnp.int32),
            vmem((2 * BLOCK, SLOTS), BF16),
            vmem((8, 8, 2, 2, 16, features), BF16),
            vmem((4, KV, BLOCK, GROUP * HEAD), BF16),
            vmem((BLOCK, features), F32),
            dma((KV, OWNERS)), dma((KV, OWNERS)),
            dma((KV, OWNERS)), dma((KV, OWNERS)),
            dma((KV, OWNERS)), dma((KV, OWNERS)),
            dma, dma((2, 2, 2, 5)), dma((2, 2, 2, 5)), dma((2, 8)), dma((2, 8)),
            dma((KV, 6)), dma((KV, 6)),
        ],
        compiler_params=pltpu.CompilerParams(
            collective_id=0, has_side_effects=True, vmem_limit_bytes=58 << 20
        ),
        cost_estimate=pl.CostEstimate(flops=7 << 30, bytes_accessed=4 << 20, transcendentals=5 << 20),
    )(queries, keys, values, picks, out_weight.reshape(2, 16, features))


def solution(mesh):
    return jax.shard_map(
        on_device,
        mesh=mesh,
        in_specs=(
            P("seq", "head"),
            P("seq", "head"),
            P("seq", "head"),
            P("seq", None),
            P("seq", "head"),
        ),
        out_specs=P("seq", "head"),
        check_vma=False,
    )
```

time: 462 us -> 182 us (0.39)
  the two profiles are of different devices: /device:TPU:1 before, /device:TPU:56 now
where the time goes in v2:
time: 182 us
  Pallas kernels  178 us (98%)
  local copies, waits for them, and re-layouts  3.8 us (2%)
    pallas_call x1, Pallas kernels, on_device(): pl.pallas_call(kernel, out_shape=jax.ShapeDtypeStruct((BLOCK, features),...  178 us
    unnamed x2, local copies, waits for them, and re-layouts  3.8 us

profile of v2, /device:TPU:56, one launch (start us, length us, event | category | flops | bytes accessed | tf_op | source)
XLA Modules:
  0.0 182.1 jit_solution(2261681097502478703)
XLA Ops:
  0.0 1.5 copy.6.picks_ref
  1.5 178.3 %shard_map.55 = bf16[512,1024]{1,0:T(8,128)(2,1)} custom-call(bf16[512,1024]{1,0:T(8,128)(2,1)} %q_ref.1, bf16[512,256]{1,0:T(8,128)(2,1)} %k_ref.1, bf16[512,256]{1,0:T(8,128)(2,1)} %v_ref.1, s32[512,2]{1,0:T(8,128)} %copy.6.picks_ref, bf16[2,16,1024]{2,1,0:T(8,128)(2,1)} %bitcast.1), custom_call_target="tpu_custom_call" | custom-call | flops 7516192768 | bytes 4194304 | tf_op jit(solution)/shard_map/pallas_call | solution.py:365
  179.8 2.3 %copy.8 = bf16[512,1024]{1,0:T(8,128)(2,1)} copy(bf16[512,1024]{1,0:T(8,128)(2,1)} %shard_map.55) | data formatting | bytes 2097152

commit v3 on v2

v3 whole, which is shorter than its diff:
```python
import functools
import math

import jax
import jax.numpy as jnp
from jax import lax
from jax.experimental import pallas as pl
from jax.experimental.pallas import tpu as pltpu
from jax.sharding import PartitionSpec as P

HEAD = 128
CAP = 6
BLOCK = 512
OWNERS = 128
GROUP = 4
KV = 2
ROWS = CAP * GROUP
SLOTS = CAP * OWNERS
BATCH = 8
STRIDE = OWNERS // BATCH
MESH = pl.DeviceIdType.MESH
F32 = jnp.float32
BF16 = jnp.bfloat16
LOG2E = 1.0 / math.log(2.0)
SCALE = LOG2E / math.sqrt(HEAD)


def dot(a, b):
    return lax.dot_general(a, b, (((1,), (0,)), ((), ())), preferred_element_type=F32)


def dot_t(a, b):
    return lax.dot_general(a, b, (((1,), (1,)), ((), ())), preferred_element_type=F32)


def loop(low, high, body):
    def step(i, carry):
        body(i)
        return carry

    lax.fori_loop(low, high, step, 0)


def iota(shape, dim):
    return lax.broadcasted_iota(jnp.int32, shape, dim)


def kernel(
    q_ref, k_ref, v_ref, picks_ref, w_ref, out_ref,
    rows32, q_out, q_in, part_out, part_in, stat_out, stat_in,
    own_out, own_peak, own_total, choose, hits, ranked, dead, full, every, total,
    q_send, q_recv, p_send, p_recv, s_send, s_recv,
    w_local, w_send, w_recv, sib_send, sib_recv, x_send, x_recv,
):
    me = lax.axis_index("seq")
    x = lax.axis_index("head")
    core = lax.rem(me, 2)
    z = lax.rem(me // 2, 8)
    y = me // 16
    right, left = lax.rem(x + 1, 4), lax.rem(x + 3, 4)

    barrier = pltpu.get_barrier_semaphore()
    loop(1, OWNERS, lambda i: pl.semaphore_signal(
        barrier, inc=1, device_id={"seq": lax.rem(me + i, OWNERS)}, device_id_type=MESH))
    for friend in (right, left):
        pl.semaphore_signal(barrier, inc=1, device_id={"head": friend}, device_id_type=MESH)

    w_copy = pltpu.make_async_copy(w_ref, full.at[y, z, core], w_local)
    w_copy.start()

    def away(p):
        return STRIDE * (p % BATCH) + p // BATCH

    def place_of(block):
        return (me - block) % STRIDE * BATCH + (me - block) // STRIDE

    first, second = picks_ref[0:1, :], picks_ref[1:2, :]
    places = iota((OWNERS, BLOCK), 0)
    owners = me - away(places)
    owners = jnp.where(owners < 0, -2, owners)
    hit0, hit1 = first == owners, second == owners
    named = jnp.where(hit0 | hit1, 1.0, 0.0).astype(BF16)
    before = jnp.where(iota((BLOCK, BLOCK), 0) < iota((BLOCK, BLOCK), 1), 1.0, 0.0).astype(BF16)
    rank = dot(named, before)
    rank0 = jnp.sum(jnp.where(hit0, rank, 0.0), axis=0, keepdims=True)
    rank1 = jnp.sum(jnp.where(hit1, rank, 0.0), axis=0, keepdims=True)
    slot0 = jnp.where(first >= 0, rank0.astype(jnp.int32) * OWNERS + place_of(first), -1)
    slot1 = jnp.where(second >= 0, rank1.astype(jnp.int32) * OWNERS + place_of(second), -1)

    def gather(j):
        for r in range(CAP):
            at = places + r * OWNERS
            pick = jnp.where((slot0 == at) | (slot1 == at), 1.0, 0.0).astype(BF16)
            got = dot(pick, q_ref[:, j * GROUP * HEAD:(j + 1) * GROUP * HEAD])
            for g in range(GROUP):
                rows32[j, pl.ds(GROUP * r + g, OWNERS, ROWS), :] = got[:, g * HEAD:(g + 1) * HEAD]

        def pack(i):
            block = rows32[j, pl.ds(pl.multiple_of(i * 16 * ROWS, 16 * ROWS), 16 * ROWS), :]
            q_out[j, pl.ds(i * 16, 16)] = block.reshape(16, ROWS, HEAD).astype(BF16)

        loop(0, OWNERS // 16, pack)

    def tables():
        line = iota((OWNERS, BLOCK), 0)
        flat = jnp.where(line == 0, first.astype(F32), jnp.where(line == 1, second.astype(F32),
               jnp.where(line == 2, rank0, jnp.where(line == 3, rank1, 0.0))))
        columns = jnp.transpose(flat)
        lane = iota((BLOCK, OWNERS), 1)
        for c in range(2):
            rows = slice(c * BLOCK, (c + 1) * BLOCK)
            name = columns[:, c:c + 1].astype(jnp.int32)
            rank = columns[:, c + 2:c + 3].astype(jnp.int32)
            place = jnp.where(name >= 0, place_of(name), -1)
            slot = jnp.where(name >= 0, rank * OWNERS + place, -1)
            for r in range(CAP):
                choose[rows, r * OWNERS:(r + 1) * OWNERS] = jnp.where(slot == lane + r * OWNERS, 1.0, 0.0).astype(BF16)
            hits[rows] = jnp.where(place == lane, 1.0, 0.0).astype(BF16)
            ranked[rows] = jnp.where(rank == lane // GROUP, 1.0, 0.0)
            dead[rows] = jnp.where(jnp.broadcast_to(name, (BLOCK, 2 * HEAD)) >= 0, 0.0, -1e30)

    def move(src, dst, send_sem, recv_sem, to):
        return pltpu.make_async_remote_copy(
            src_ref=src, dst_ref=dst, send_sem=send_sem, recv_sem=recv_sem,
            device_id=to, device_id_type=MESH)

    def sender(out, into, send, recv, way):
        def copy(j, p):
            return move(out.at[j, p], into.at[j, p], send.at[j, p // BATCH], recv.at[j, p // BATCH],
                        {"seq": me + way * away(p)})
        return copy

    def waiter(out, into, send, recv):
        def wait(j, n, low, high, sent):
            for count in range(1, BATCH + 1):
                @pl.when(high - low == count)
                def _():
                    some = pl.ds(low, count)
                    copy = move(out.at[j, some], into.at[j, some], send.at[j, n], recv.at[j, n],
                                {"seq": lax.rem(me + 1, OWNERS)})
                    if sent:
                        copy.wait_send()
                    else:
                        copy.wait_recv()
        return wait

    query_sems = (q_out, q_in, q_send, q_recv)
    part_sems = (part_out, part_in, p_send, p_recv)
    stat_sems = (stat_out, stat_in, s_send, s_recv)
    query, query_wait = sender(*query_sems, -1), waiter(*query_sems)
    part, part_wait = sender(*part_sems, 1), waiter(*part_sems)
    stat, stat_wait = sender(*stat_sems, 1), waiter(*stat_sems)

    groups = OWNERS // BATCH

    def live(n, devices):
        return n * BATCH + jnp.where(n == 0, 1, 0), n * BATCH + (devices - n + STRIDE) // STRIDE

    def for_earlier(body):
        loop(0, groups, lambda n: body(n, *live(n, me)))

    def for_later(body):
        loop(0, groups, lambda n: body(n, *live(n, OWNERS - 1 - me)))

    def send_queries(j):
        for_earlier(lambda n, low, high: loop(low, high, lambda p: query(j, p).start()))

    def device(yy, zz, cc):
        return {"seq": (yy * 8 + zz) * 2 + cc}

    def w_unit(phase, h, p, c):
        if phase == 0:
            return full.at[y, p, c, h] if h == 0 else full.at[p, z, c, h]
        return full.at[p, :, c, h] if h == 0 else full.at[:, p, c, h]

    def w_move(phase, h, step, way):
        along_z = (h == 0) == (phase == 0)
        pos = z if along_z else y
        ahead = lax.rem(pos + 8 + way, 8)
        unit = w_unit(phase, h, lax.rem(pos - way * (step - 1) + 8, 8), core)
        to = device(y, ahead, core) if along_z else device(ahead, z, core)
        i = 0 if way > 0 else 1
        return move(unit, unit, w_send.at[phase, h, i, step - 1], w_recv.at[phase, h, i, step - 1], to)

    def sibling(h, p, c):
        unit = w_unit(1, h, p, c)
        return move(unit, unit, sib_send.at[h, p], sib_recv.at[h, p], device(y, z, 1 - core))

    def w_moves(phase, step):
        ways = (1, -1) if step < 4 else (1,)
        return [(h, way, w_move(phase, h, step, way)) for way in ways for h in range(2)]

    def w_start(phase, step):
        if phase == 1 and step == 1:
            for h in range(2):
                sibling(h, (y, z)[h], core).start()
        for _, _, copy in w_moves(phase, step):
            copy.start()

    def w_wait(phase, step):
        for h, way, copy in w_moves(phase, step):
            copy.wait_recv()
            if phase == 1:
                sibling(h, lax.rem((y, z)[h] - way * step + 8, 8), core).start()

    def w_next(phase, step):
        w_wait(phase, step)
        if step < 4:
            w_start(phase, step + 1)
        elif phase == 0:
            w_start(1, 1)

    def own(h):
        j = h // GROUP
        cols = slice(h * HEAD, (h + 1) * HEAD)
        for part_no in range(2):
            rows = slice(part_no * 256, part_no * 256 + 256)
            keys = (part_no + 1) * 256
            s = dot_t(q_ref[rows, cols], k_ref[0:keys, j * HEAD:(j + 1) * HEAD])
            seen = iota((256, keys), 1) <= iota((256, keys), 0) + part_no * 256
            s = jnp.where(seen, s, -1e30)
            peak = jnp.max(s, axis=1, keepdims=True)
            weights = jnp.exp2((s - peak) * SCALE)
            own_peak[rows, cols] = jnp.broadcast_to(peak * SCALE, (256, HEAD))
            own_total[rows, cols] = jnp.broadcast_to(jnp.sum(weights, axis=1, keepdims=True), (256, HEAD))
            own_out[rows, cols] = dot(weights.astype(BF16), v_ref[0:keys, j * HEAD:(j + 1) * HEAD])

    def remote(j, n):
        base = n * BATCH
        low, high = live(n, OWNERS - 1 - me)
        query_wait(j, n, low, high, False)
        batch = pl.ds(base, BATCH)
        rows = q_in[j, batch].astype(F32).reshape(BATCH * ROWS, HEAD).astype(BF16)
        s = dot_t(rows, k_ref[:, j * HEAD:(j + 1) * HEAD])
        peak = jnp.max(s, axis=1, keepdims=True)
        weights = jnp.exp2((s - peak) * SCALE)
        mass = jnp.sum(weights, axis=1, keepdims=True)
        mixed = dot(weights.astype(BF16), v_ref[:, j * HEAD:(j + 1) * HEAD]) * (1.0 / mass)
        part_out[j, batch] = mixed.reshape(BATCH, ROWS, HEAD).astype(BF16)
        level = peak * SCALE + jnp.log(mass) * LOG2E
        level = jnp.broadcast_to(level, (BATCH * ROWS, HEAD)).reshape(BATCH, ROWS, HEAD)
        diagonal = iota(level.shape, 1) == iota(level.shape, 2)
        stat_out[j, batch] = jnp.sum(jnp.where(diagonal, level, 0.0), axis=1, keepdims=True)

        def answer(d):
            part(j, d).start()
            stat(j, d).start()

        loop(low, high, answer)

    def remote_some(j, i, count):
        loop(groups * i // count, groups * (i + 1) // count, lambda n: remote(j, n))

    def combine(j):
        def arrived(n, low, high):
            part_wait(j, n, low, high, False)
            stat_wait(j, n, low, high, False)

        for_earlier(arrived)

        def widen(i):
            block = part_in[j, pl.ds(i * 16, 16)].astype(F32)
            gap = away(iota(block.shape, 0) + i * 16)
            block = jnp.where((gap > 0) & (gap <= me), block, 0.0)
            rows32[j, pl.ds(pl.multiple_of(i * 16 * ROWS, 16 * ROWS), 16 * ROWS), :] = block.reshape(16 * ROWS, HEAD)

        loop(0, OWNERS // 16, widen)
        levels = jnp.sum(stat_in[j], axis=1)
        gap = away(iota(levels.shape, 0))
        levels = jnp.where((gap > 0) & (gap <= me), levels, 0.0)
        high = levels.astype(BF16)
        rest = levels - high.astype(F32)
        mid = rest.astype(BF16)
        low = (rest - mid.astype(F32)).astype(BF16)
        found = [(dot(hits[...], piece) * ranked[...]).astype(BF16) for piece in (high, mid, low)]
        for pair in range(GROUP // 2):
            lane, head = iota((HEAD, 2 * HEAD), 0), iota((HEAD, 2 * HEAD), 1) // HEAD + 2 * pair
            spread = jnp.where((lane % GROUP == head) & (lane < ROWS), 1.0, 0.0).astype(BF16)
            source = jnp.concatenate([jnp.concatenate(
                [rows32[j, pl.ds(GROUP * r + 2 * pair + i, OWNERS, ROWS), :].astype(BF16) for i in range(2)],
                axis=1) for r in range(CAP)], axis=0)
            cols = slice((j * GROUP + 2 * pair) * HEAD, (j * GROUP + 2 * pair + 2) * HEAD)
            for half in range(2):
                rows = slice(half * 256, half * 256 + 256)
                got, level = [], []
                for c in range(2):
                    some = slice(c * BLOCK + half * 256, c * BLOCK + half * 256 + 256)
                    got.append(dot(choose[some], source))
                    level.append(sum(dot(piece[some], spread) for piece in found) + dead[some])
                peak = own_peak[rows, cols]
                top = jnp.maximum(peak, jnp.maximum(level[0], level[1]))
                own_share = jnp.exp2(peak - top)
                share = [jnp.exp2(level[c] - top) for c in range(2)]
                norm = 1.0 / (own_share * own_total[rows, cols] + share[0] + share[1])
                mixed = own_out[rows, cols] * own_share + got[0] * share[0] + got[1] * share[1]
                every[x, j, rows, 2 * pair * HEAD:(2 * pair + 2) * HEAD] = (mixed * norm).astype(BF16)

    upper, lower = pl.ds(0, BLOCK // 2), pl.ds(BLOCK // 2, BLOCK // 2)

    def x_move(j, i, owner, rows, to):
        unit = every.at[owner, j, rows]
        return move(unit, unit, x_send.at[j, i], x_recv.at[j, i], {"head": to})

    def x_copies(j):
        return [
            x_move(j, 0, x, upper, right), x_move(j, 1, x, lower, left),
            x_move(j, 2, x, lower, right), x_move(j, 3, x, upper, left),
        ]

    def x_onward(j):
        return [x_move(j, 4, left, upper, right), x_move(j, 5, right, lower, left)]

    def x_start(j):
        for copy in x_copies(j):
            copy.start()

    def x_forward(j):
        copies, onward = x_copies(j), x_onward(j)
        for i in range(2):
            copies[i].wait_recv()
            onward[i].start()

    def project(owner, j, first_term):
        a = every[owner, j]
        for n in range(4):
            cols = slice(n * 256, n * 256 + 256)
            w = full[2 * owner + j, :, :, :, :, cols].reshape(BLOCK, 256)
            term = dot(a, w)
            total[:, cols] = term if first_term else total[:, cols] + term

    def w_finish():
        for phase in range(2):
            for step in range(1, 5):
                for _, _, copy in w_moves(phase, step):
                    copy.wait_send()
        for h in range(2):
            for p in range(8):
                sibling(h, p, 1 - core).wait_recv()
                sibling(h, p, core).wait_send()

    def all_sent():
        def queries_sent(n, low, high):
            for j in range(KV):
                query_wait(j, n, low, high, True)

        def parts_sent(n, low, high):
            for j in range(KV):
                part_wait(j, n, low, high, True)
                stat_wait(j, n, low, high, True)

        for_earlier(queries_sent)
        for_later(parts_sent)

    gather(0)
    w_copy.wait()
    pl.semaphore_wait(barrier, OWNERS + 1)
    send_queries(0)
    w_start(0, 1)
    gather(1)
    send_queries(1)
    w_next(0, 1)
    tables()
    w_next(0, 2)
    for h in range(KV * GROUP):
        own(h)
        if h in (1, 4):
            w_next(0, 3 if h == 1 else 4)
    remote_some(0, 0, 1)
    w_next(1, 1)
    remote_some(1, 0, 1)
    w_next(1, 2)
    combine(0)
    x_start(0)
    w_next(1, 3)
    x_forward(0)
    combine(1)
    x_start(1)
    w_wait(1, 4)
    w_finish()
    for copy in x_copies(0)[2:] + x_onward(0):
        copy.wait_recv()
    project(x, 0, True)
    project(left, 0, False)
    project(right, 0, False)
    x_forward(1)
    project(lax.rem(x + 2, 4), 0, False)
    project(x, 1, False)
    all_sent()
    for copy in x_copies(1)[2:]:
        copy.wait_recv()
    project(left, 1, False)
    project(right, 1, False)
    for copy in x_onward(1):
        copy.wait_recv()
    project(lax.rem(x + 2, 4), 1, False)
    out_ref[...] = total[...].astype(BF16)
    for j in range(KV):
        for copy in x_copies(j) + x_onward(j):
            copy.wait_send()


def on_device(queries, keys, values, picks, out_weight):
    vmem, dma = pltpu.VMEM, pltpu.SemaphoreType.DMA
    features = out_weight.shape[1]
    return pl.pallas_call(
        kernel,
        out_shape=jax.ShapeDtypeStruct((BLOCK, features), BF16),
        in_specs=[pl.BlockSpec(memory_space=vmem)] * 5,
        out_specs=pl.BlockSpec(memory_space=vmem),
        scratch_shapes=[
            vmem((KV, OWNERS * ROWS, HEAD), F32),
            vmem((KV, OWNERS, ROWS, HEAD), BF16),
            vmem((KV, OWNERS, ROWS, HEAD), BF16),
            vmem((KV, OWNERS, ROWS, HEAD), BF16),
            vmem((KV, OWNERS, ROWS, HEAD), BF16),
            vmem((KV, OWNERS, 1, HEAD), F32),
            vmem((KV, OWNERS, 1, HEAD), F32),
            vmem((BLOCK, KV * GROUP * HEAD), F32),
            vmem((BLOCK, KV * GROUP * HEAD), F32),
            vmem((BLOCK, KV * GROUP * HEAD), F32),
            vmem((2 * BLOCK, SLOTS), BF16),
            vmem((2 * BLOCK, OWNERS), BF16),
            vmem((2 * BLOCK, OWNERS), F32),
            vmem((2 * BLOCK, 2 * HEAD), F32),
            vmem((8, 8, 2, 2, 16, features), BF16),
            vmem((4, KV, BLOCK, GROUP * HEAD), BF16),
            vmem((BLOCK, features), F32),
            dma((KV, OWNERS // BATCH)), dma((KV, OWNERS // BATCH)),
            dma((KV, OWNERS // BATCH)), dma((KV, OWNERS // BATCH)),
            dma((KV, OWNERS // BATCH)), dma((KV, OWNERS // BATCH)),
            dma, dma((2, 2, 2, 4)), dma((2, 2, 2, 4)), dma((2, 8)), dma((2, 8)),
            dma((KV, 6)), dma((KV, 6)),
        ],
        compiler_params=pltpu.CompilerParams(
            collective_id=0, has_side_effects=True, vmem_limit_bytes=58 << 20
        ),
        cost_estimate=pl.CostEstimate(flops=7 << 30, bytes_accessed=4 << 20, transcendentals=5 << 20),
    )(queries, keys, values, picks.T, out_weight.reshape(2, 16, features))


def solution(mesh):
    return jax.shard_map(
        on_device,
        mesh=mesh,
        in_specs=(
            P("seq", "head"),
            P("seq", "head"),
            P("seq", "head"),
            P("seq", None),
            P("seq", "head"),
        ),
        out_specs=P("seq", "head"),
        check_vma=False,
    )
```

time: 182 us -> 159 us (0.87)
  Pallas kernels: 178 us -> 156 us
    pallas_call x1, Pallas kernels: 178 us -> 156 us  [on_device(): pl.pallas_call(kernel, out_shape=jax.ShapeDtypeStruct((BLOCK, features),...]
    unnamed x2 -> x1, local copies, waits for them, and re-layouts: 3.8 us -> 2.26 us
where the time goes in v3:
time: 159 us
  Pallas kernels  156 us (98%)
  local copies, waits for them, and re-layouts  2.26 us (1%)
    pallas_call x1, Pallas kernels, on_device(): pl.pallas_call(kernel, out_shape=jax.ShapeDtypeStruct((BLOCK, features),...  156 us

profile of v3, /device:TPU:56, one launch (start us, length us, event | category | flops | bytes accessed | tf_op | source)
XLA Modules:
  0.0 158.6 jit_solution(14662130704139324330)
XLA Ops:
  0.0 156.3 %shard_map.55 = bf16[512,1024]{1,0:T(8,128)(2,1)} custom-call(bf16[512,1024]{1,0:T(8,128)(2,1)} %q_ref.1, bf16[512,256]{1,0:T(8,128)(2,1)} %k_ref.1, bf16[512,256]{1,0:T(8,128)(2,1)} %v_ref.1, s32[2,512]{1,0:T(2,128)} %bitcast.3, bf16[2,16,1024]{2,1,0:T(8,128)(2,1)} %bitcast.2), custom_call_target="tpu_custom_call" | custom-call | flops 7516192768 | bytes 4194304 | tf_op jit(solution)/shard_map/pallas_call | solution.py:405
  156.3 2.3 %copy.7 = bf16[512,1024]{1,0:T(8,128)(2,1)} copy(bf16[512,1024]{1,0:T(8,128)(2,1)} %shard_map.55) | data formatting | bytes 2097152

commit v4 on v3

--- a/solution.py
+++ b/solution.py
@@ -358,17 +358,17 @@
     w_start(0, 1)
     gather(1)
     send_queries(1)
-    w_next(0, 1)
-    tables()
-    w_next(0, 2)
-    for h in range(KV * GROUP):
-        own(h)
-        if h in (1, 4):
-            w_next(0, 3 if h == 1 else 4)
-    remote_some(0, 0, 1)
-    w_next(1, 1)
-    remote_some(1, 0, 1)
-    w_next(1, 2)
+    for i in range(4):
+        remote_some(0, i, 4)
+        w_next(0, i + 1)
+    for i in range(4):
+        remote_some(1, i, 4)
+        own(2 * i)
+        own(2 * i + 1)
+        if i == 0:
+            tables()
+        if i in (1, 3):
+            w_next(1, 1 + i // 2)
     combine(0)
     x_start(0)
     w_next(1, 3)

time: 159 us -> 155 us (0.975)
  Pallas kernels: 156 us -> 152 us
    pallas_call x1, Pallas kernels: 156 us -> 152 us  [on_device(): pl.pallas_call(kernel, out_shape=jax.ShapeDtypeStruct((BLOCK, features),...]
where the time goes in v4:
time: 155 us
  Pallas kernels  152 us (98%)
  local copies, waits for them, and re-layouts  2.26 us (1%)
    pallas_call x1, Pallas kernels, on_device(): pl.pallas_call(kernel, out_shape=jax.ShapeDtypeStruct((BLOCK, features),...  152 us

profile of v4, /device:TPU:56, one launch (start us, length us, event | category | flops | bytes accessed | tf_op | source)
XLA Modules:
  0.0 154.7 jit_solution(7485274737387076351)
XLA Ops:
  0.0 152.4 %shard_map.55 = bf16[512,1024]{1,0:T(8,128)(2,1)} custom-call(bf16[512,1024]{1,0:T(8,128)(2,1)} %q_ref.1, bf16[512,256]{1,0:T(8,128)(2,1)} %k_ref.1, bf16[512,256]{1,0:T(8,128)(2,1)} %v_ref.1, s32[2,512]{1,0:T(2,128)} %bitcast.3, bf16[2,16,1024]{2,1,0:T(8,128)(2,1)} %bitcast.2), custom_call_target="tpu_custom_call" | custom-call | flops 7516192768 | bytes 4194304 | tf_op jit(solution)/shard_map/pallas_call | solution.py:405
  152.4 2.3 %copy.7 = bf16[512,1024]{1,0:T(8,128)(2,1)} copy(bf16[512,1024]{1,0:T(8,128)(2,1)} %shard_map.55) | data formatting | bytes 2097152

commit v5 on v4

--- a/solution.py
+++ b/solution.py
@@ -250,6 +250,31 @@
 
     def remote_some(j, i, count):
         loop(groups * i // count, groups * (i + 1) // count, lambda n: remote(j, n))
+
+    upper, lower = pl.ds(0, BLOCK // 2), pl.ds(BLOCK // 2, BLOCK // 2)
+
+    def x_move(j, pair, i, owner, rows, to):
+        unit = every.at[owner, j, rows, pl.ds(2 * pair * HEAD, 2 * HEAD)]
+        return move(unit, unit, x_send.at[j, pair, i], x_recv.at[j, pair, i], {"head": to})
+
+    def x_first(j, pair):
+        return [x_move(j, pair, 0, x, upper, right), x_move(j, pair, 1, x, lower, left)]
+
+    def x_second(j, pair):
+        return [x_move(j, pair, 2, x, lower, right), x_move(j, pair, 3, x, upper, left)]
+
+    def x_onward(j, pair):
+        return [x_move(j, pair, 4, left, upper, right), x_move(j, pair, 5, right, lower, left)]
+
+    def x_start(j, pair):
+        for copy in x_first(j, pair) + x_second(j, pair):
+            copy.start()
+
+    def x_forward(j):
+        for pair in range(2):
+            for here, onward in zip(x_first(j, pair), x_onward(j, pair)):
+                here.wait_recv()
+                onward.start()
 
     def combine(j):
         def arrived(n, low, high):
@@ -294,31 +319,7 @@
                 norm = 1.0 / (own_share * own_total[rows, cols] + share[0] + share[1])
                 mixed = own_out[rows, cols] * own_share + got[0] * share[0] + got[1] * share[1]
                 every[x, j, rows, 2 * pair * HEAD:(2 * pair + 2) * HEAD] = (mixed * norm).astype(BF16)
-
-    upper, lower = pl.ds(0, BLOCK // 2), pl.ds(BLOCK // 2, BLOCK // 2)
-
-    def x_move(j, i, owner, rows, to):
-        unit = every.at[owner, j, rows]
-        return move(unit, unit, x_send.at[j, i], x_recv.at[j, i], {"head": to})
-
-    def x_copies(j):
-        return [
-            x_move(j, 0, x, upper, right), x_move(j, 1, x, lower, left),
-            x_move(j, 2, x, lower, right), x_move(j, 3, x, upper, left),
-        ]
-
-    def x_onward(j):
-        return [x_move(j, 4, left, upper, right), x_move(j, 5, right, lower, left)]
-
-    def x_start(j):
-        for copy in x_copies(j):
-            copy.start()
-
-    def x_forward(j):
-        copies, onward = x_copies(j), x_onward(j)
-        for i in range(2):
-            copies[i].wait_recv()
-            onward[i].start()
+            x_start(j, pair)
 
     def project(owner, j, first_term):
         a = every[owner, j]
@@ -370,15 +371,14 @@
         if i in (1, 3):
             w_next(1, 1 + i // 2)
     combine(0)
-    x_start(0)
     w_next(1, 3)
     x_forward(0)
     combine(1)
-    x_start(1)
     w_wait(1, 4)
     w_finish()
-    for copy in x_copies(0)[2:] + x_onward(0):
-        copy.wait_recv()
+    for pair in range(2):
+        for copy in x_second(0, pair) + x_onward(0, pair):
+            copy.wait_recv()
     project(x, 0, True)
     project(left, 0, False)
     project(right, 0, False)
@@ -386,17 +386,20 @@
     project(lax.rem(x + 2, 4), 0, False)
     project(x, 1, False)
     all_sent()
-    for copy in x_copies(1)[2:]:
-        copy.wait_recv()
+    for pair in range(2):
+        for copy in x_second(1, pair):
+            copy.wait_recv()
     project(left, 1, False)
     project(right, 1, False)
-    for copy in x_onward(1):
-        copy.wait_recv()
+    for pair in range(2):
+        for copy in x_onward(1, pair):
+            copy.wait_recv()
     project(lax.rem(x + 2, 4), 1, False)
     out_ref[...] = total[...].astype(BF16)
     for j in range(KV):
-        for copy in x_copies(j) + x_onward(j):
-            copy.wait_send()
+        for pair in range(2):
+            for copy in x_first(j, pair) + x_second(j, pair) + x_onward(j, pair):
+                copy.wait_send()
 
 
 def on_device(queries, keys, values, picks, out_weight):
@@ -429,7 +432,7 @@
             dma((KV, OWNERS // BATCH)), dma((KV, OWNERS // BATCH)),
             dma((KV, OWNERS // BATCH)), dma((KV, OWNERS // BATCH)),
             dma, dma((2, 2, 2, 4)), dma((2, 2, 2, 4)), dma((2, 8)), dma((2, 8)),
-            dma((KV, 6)), dma((KV, 6)),
+            dma((KV, 2, 6)), dma((KV, 2, 6)),
         ],
         compiler_params=pltpu.CompilerParams(
             collective_id=0, has_side_effects=True, vmem_limit_bytes=58 << 20

time: 155 us -> 154 us (level)
  no operation moved by 1% of the time
where the time goes in v5:
time: 154 us
  Pallas kernels  152 us (99%)
  local copies, waits for them, and re-layouts  2.26 us (1%)
    pallas_call x1, Pallas kernels, on_device(): pl.pallas_call(kernel, out_shape=jax.ShapeDtypeStruct((BLOCK, features),...  152 us

profile of v5, /device:TPU:56, one launch (start us, length us, event | category | flops | bytes accessed | tf_op | source)
XLA Modules:
  0.0 154.3 jit_solution(9785897821530344254)
XLA Ops:
  0.0 152.0 %shard_map.55 = bf16[512,1024]{1,0:T(8,128)(2,1)} custom-call(bf16[512,1024]{1,0:T(8,128)(2,1)} %q_ref.1, bf16[512,256]{1,0:T(8,128)(2,1)} %k_ref.1, bf16[512,256]{1,0:T(8,128)(2,1)} %v_ref.1, s32[2,512]{1,0:T(2,128)} %bitcast.3, bf16[2,16,1024]{2,1,0:T(8,128)(2,1)} %bitcast.2), custom_call_target="tpu_custom_call" | custom-call | flops 7516192768 | bytes 4194304 | tf_op jit(solution)/shard_map/pallas_call | solution.py:408
  152.0 2.3 %copy.7 = bf16[512,1024]{1,0:T(8,128)(2,1)} copy(bf16[512,1024]{1,0:T(8,128)(2,1)} %shard_map.55) | data formatting | bytes 2097152
